TPU v7x, 256 devices: a whole 4x4x8 slice. The times are simulated.
256 devices in a mesh: context: 64 (over x, z_lo, y), tensor: 4 (over z_hi, core).
Axes of the slice: x: 4, y: 4, z: 8 (z_hi: 2, z_lo: 4; z = z_hi * 4 + z_lo), core: 2. Of those that a mesh axis runs over, the one named last changes fastest.
Arguments:
- queries: bfloat16 [16384, 4096], P('context', 'tensor'), may hold values from -6 to 6
- keys: bfloat16 [16384, 4096], P('context', 'tensor'), may hold values from -6 to 6
- values: bfloat16 [16384, 4096], P('context', 'tensor'), may hold values from -6 to 6
- cotangent: bfloat16 [16384, 4096], P('context', 'tensor'), may hold values from -6 to 6
- filter_param: bfloat16 [16384, 1024], P('context'), may hold values from -120 to 120
- skip: float32 [4096], P('tensor'), may hold values from 0.5 to 1.5
Outputs:
- output: bfloat16 [16384, 4096], P('context', 'tensor')
- d_queries: bfloat16 [16384, 4096], P('context', 'tensor')
- d_keys: bfloat16 [16384, 4096], P('context', 'tensor')
- d_values: bfloat16 [16384, 4096], P('context', 'tensor')
- filter_grad: float32 [16384, 1024], P(('context', 'tensor'))
All inputs are finite; a program needn't handle non-finite values.
Results may differ from a plain program's by a relative error of at most 0.014.
Values may be sent and summed in bfloat16 or wider, within the bound.
A program may use at most 128 MiB of HBM per device.

v0:
```python
import math

import jax
import jax.numpy as jnp
from jax import lax
from jax.sharding import PartitionSpec as P


def factor_length(seq_len):
    inner = math.isqrt(2 * seq_len)
    while seq_len % inner != 0:
        inner -= 1
    return (inner, 2 * seq_len // inner)


def angle_table(row_count, col_count, period):
    row_index = jnp.arange(row_count, dtype=jnp.int32)[:, None]
    col_index = jnp.arange(col_count, dtype=jnp.int32)[None, :]
    phase = (row_index * col_index % period).astype(jnp.float32) * (-2.0 * math.pi / period)
    return (jnp.cos(phase), jnp.sin(phase))


def contract(form, table, operand):
    return jnp.einsum(
        form, table, operand, precision=lax.Precision.HIGHEST, preferred_element_type=jnp.float32
    )


def forward_real(signal, tables, inner, outer):
    (outer_cos, outer_sin), (twist_cos, twist_sin), (inner_cos, inner_sin) = tables
    shaped = signal.reshape(signal.shape[0], outer // 2, inner)
    first_re = contract("kn,cnm->ckm", outer_cos, shaped)
    first_im = contract("kn,cnm->ckm", outer_sin, shaped)
    turned_re = first_re * twist_cos - first_im * twist_sin
    turned_im = first_re * twist_sin + first_im * twist_cos
    spec_re = contract("jm,ckm->cjk", inner_cos, turned_re) - contract(
        "jm,ckm->cjk", inner_sin, turned_im
    )
    spec_im = contract("jm,ckm->cjk", inner_cos, turned_im) + contract(
        "jm,ckm->cjk", inner_sin, turned_re
    )
    return (spec_re, spec_im)


def inverse(spec_re, spec_im, tables, inner, outer, want_imag):
    (outer_cos, outer_sin), (twist_cos, twist_sin), (inner_cos, inner_sin) = tables
    channels = spec_re.shape[0]
    factor = 1.0 / (inner * outer)
    first_re = contract("jm,cjk->ckm", inner_cos, spec_re) + contract(
        "jm,cjk->ckm", inner_sin, spec_im
    )
    first_im = contract("jm,cjk->ckm", inner_cos, spec_im) - contract(
        "jm,cjk->ckm", inner_sin, spec_re
    )
    turned_re = first_re * twist_cos + first_im * twist_sin
    turned_im = first_im * twist_cos - first_re * twist_sin
    real_part = contract("kn,ckm->cnm", outer_cos, turned_re) + contract(
        "kn,ckm->cnm", outer_sin, turned_im
    )
    real_part = real_part.reshape(channels, -1) * factor
    if want_imag:
        imag_part = contract("kn,ckm->cnm", outer_cos, turned_im) - contract(
            "kn,ckm->cnm", outer_sin, turned_re
        )
        return (real_part, imag_part.reshape(channels, -1) * factor)
    return real_part


def shards(queries, keys, values, cotangent, filter_param, skip):
    rows, width = queries.shape
    groups = lax.axis_size("context")
    seq_len = rows * groups
    scale = 1.0 / math.sqrt(seq_len)
    inner, outer = factor_length(seq_len)
    tables = (
        angle_table(outer, outer // 2, outer),
        angle_table(outer, inner, inner * outer),
        angle_table(inner, inner, inner),
    )
    gated = (keys.astype(jnp.float32) * values.astype(jnp.float32)).astype(jnp.bfloat16)
    grad_in = (queries.astype(jnp.float32) * cotangent.astype(jnp.float32)).astype(jnp.bfloat16)
    gated_chan, filter_chan = (
        lax.all_to_all(gated.T, "context", split_axis=0, concat_axis=1, tiled=True),
        lax.all_to_all(filter_param.T, "context", split_axis=0, concat_axis=1, tiled=True),
    )
    taps_spec = forward_real(filter_chan.astype(jnp.float32) * scale, tables, inner, outer)
    taps_re, taps_im = taps_spec
    gated_re, gated_im = forward_real(gated_chan.astype(jnp.float32), tables, inner, outer)
    prod_re = gated_re * taps_re - gated_im * taps_im
    prod_im = gated_re * taps_im + gated_im * taps_re
    conv = inverse(prod_re, prod_im, tables, inner, outer, False).astype(jnp.bfloat16)
    gated_spec, conv = ((gated_re, gated_im), conv)
    conv_seq = lax.all_to_all(conv, "context", split_axis=1, concat_axis=0, tiled=True)
    grad_chan = lax.all_to_all(grad_in.T, "context", split_axis=0, concat_axis=1, tiled=True)
    gated_re, gated_im = gated_spec
    taps_re, taps_im = taps_spec
    grad_re, grad_im = forward_real(grad_chan.astype(jnp.float32), tables, inner, outer)
    back_re = taps_re * grad_re + taps_im * grad_im
    back_im = taps_re * grad_im - taps_im * grad_re
    corr_re = gated_re * grad_re + gated_im * grad_im
    corr_im = gated_re * grad_im - gated_im * grad_re
    back, corr = inverse(back_re - corr_im, back_im + corr_re, tables, inner, outer, True)
    back, corr = (back.astype(jnp.bfloat16), corr * scale)
    back_seq = lax.all_to_all(back, "context", split_axis=1, concat_axis=0, tiled=True)
    moved = lax.all_to_all(
        corr.astype(jnp.bfloat16), "context", split_axis=1, concat_axis=0, tiled=True
    ).astype(corr.dtype)
    collected = lax.psum_scatter(
        moved.astype(jnp.bfloat16), "tensor", scatter_dimension=1, tiled=True
    ).astype(jnp.float32)
    filter_grad = collected.T
    mixed = conv_seq.T.astype(jnp.float32) + skip * gated.astype(jnp.float32)
    output = (queries.astype(jnp.float32) * mixed).astype(jnp.bfloat16)
    d_queries = (cotangent.astype(jnp.float32) * mixed).astype(jnp.bfloat16)
    d_gated = back_seq.T.astype(jnp.float32) + skip * grad_in.astype(jnp.float32)
    d_keys = (d_gated * values.astype(jnp.float32)).astype(jnp.bfloat16)
    d_values = (d_gated * keys.astype(jnp.float32)).astype(jnp.bfloat16)
    return (output, d_queries, d_keys, d_values, filter_grad)


def solution(mesh):
    placed = (
        P("context", "tensor"),
        P("context", "tensor"),
        P("context", "tensor"),
        P("context", "tensor"),
        P("context", None),
        P("tensor"),
    )
    return jax.shard_map(
        shards,
        mesh=mesh,
        in_specs=placed,
        out_specs=(
            P("context", "tensor"),
            P("context", "tensor"),
            P("context", "tensor"),
            P("context", "tensor"),
            P(("context", "tensor"), None),
        ),
        check_vma=False,
    )
```

profile of v0, /device:TPU:1, one launch (start us, length us, event | category | flops | bytes accessed | tf_op | source)
XLA Modules:
  0.0 278.6 jit_solution(2558945900431917601)
XLA Ops:
  7.2 1.3 copy.80
  8.5 1.4 copy.81
  10.4 1.1 fusion.62
  11.5 29.7 %all_to_all.81 = bf16[64,16,256]{2,1,0:T(8,128)(2,1)S(1)} all-to-all(bf16[64,16,256]{2,1,0:T(8,128)(2,1)S(1)} %bitcast.220), channel_id=1, replica_groups=mesh['context'=64,'tensor'=4] {'context'}, dimensions={0} | all-to-all | bytes 1048576 | tf_op jit(solution)/shard_map/all_to_all | solution.py:94
  41.2 5.3 %all-to-all-start = ((bf16[64,16,256]{2,1,0:T(8,128)(2,1)}), bf16[64,16,256]{2,1,0:T(8,128)(2,1)S(1)}, u32[]{:S(2)}, u32[]{:S(2)}) async-start(bf16[64,16,256]{2,1,0:T(8,128)(2,1)} %bitcast.1), calls=%async_computation | async-start | bytes 1048576 | tf_op jit(solution)/shard_map/all_to_all | solution.py:83
  47.8 1.0 copy.90
  49.1 14.4 %all-to-all-done = bf16[64,16,256]{2,1,0:T(8,128)(2,1)S(1)} async-done(((bf16[64,16,256]{2,1,0:T(8,128)(2,1)}), bf16[64,16,256]{2,1,0:T(8,128)(2,1)S(1)}, u32[]{:S(2)}, u32[]{:S(2)}) %all-to-all-start) | async-done | bytes 524320 | tf_op jit(solution)/shard_map/all_to_all | solution.py:83
  63.6 6.3 %all-to-all-start.1 = ((bf16[64,16,256]{2,1,0:T(8,128)(2,1)}), bf16[64,16,256]{2,1,0:T(8,128)(2,1)}, u32[]{:S(2)}, u32[]{:S(2)}) async-start(bf16[64,16,256]{2,1,0:T(8,128)(2,1)} %bitcast.10), calls=%async_computation.1 | async-start | bytes 1048576 | tf_op jit(solution)/shard_map/all_to_all | solution.py:84
  70.2 1.5 fusion.101
  71.8 2.9 %fusion.110 = f32[16,128,256]{2,1,0:T(8,128)} fusion(bf16[16,128,128]{2,1,0:T(8,128)(2,1)S(1)} %reshape.97), kind=kOutput, calls=%fused_computation.123 | convolution fusion | flops 805765120 | bytes 2621440 | tf_op jit(solution)/shard_map/kn,cnm->ckm/dot_general | solution.py:24
  74.6 2.8 %fusion.96 = f32[16,128,256]{2,1,0:T(8,128)} fusion(bf16[16,128,128]{2,1,0:T(8,128)(2,1)S(1)} %reshape.98), kind=kOutput, calls=%fused_computation.109 | convolution fusion | flops 805765120 | bytes 2621440 | tf_op jit(solution)/shard_map/kn,cnm->ckm/dot_general | solution.py:24
  77.5 2.9 %fusion.105 = f32[16,128,256]{2,1,0:T(8,128)} fusion(bf16[16,128,128]{2,1,0:T(8,128)(2,1)S(1)} %reshape.98), kind=kOutput, calls=%fused_computation.118 | convolution fusion | flops 805765120 | bytes 2621440 | tf_op jit(solution)/shard_map/kn,cnm->ckm/dot_general | solution.py:24
  80.3 5.8 %all-to-all-done.1 = bf16[64,16,256]{2,1,0:T(8,128)(2,1)} async-done(((bf16[64,16,256]{2,1,0:T(8,128)(2,1)}), bf16[64,16,256]{2,1,0:T(8,128)(2,1)}, u32[]{:S(2)}, u32[]{:S(2)}) %all-to-all-start.1) | async-done | bytes 524320 | tf_op jit(solution)/shard_map/all_to_all | solution.py:84
  86.2 1.2 multiply_bitcast_fusion
  87.3 1.6 copy.91
  88.9 1.3 mul.755
  90.2 2.3 fusion.99
  92.5 2.5 fusion.108
  95.0 3.9 %fusion.78 = f32[16,256,128]{2,1,0:T(8,128)S(1)} fusion(f32[16,128,256]{2,1,0:T(8,128)S(1)} %fusion.99, f32[16,128,256]{2,1,0:T(8,128)S(1)} %fusion.108, f32[256,128]{0,1:T(8,128)S(1)} %copy.87, f32[256,128]{0,1:T(8,128)S(1)} %copy.85), kind=kOutput, calls=%fused_computation.93 | convolution fusion | flops 807108608 | bytes 6553600 | tf_op jit(solution)/shard_map/jm,ckm->cjk/dot_general | solution.py:24
  98.9 3.9 %fusion.82 = f32[16,256,128]{2,1,0:T(8,128)S(1)} fusion(f32[16,128,256]{2,1,0:T(8,128)S(1)} %fusion.99, f32[16,128,256]{2,1,0:T(8,128)S(1)} %fusion.108, f32[256,128]{0,1:T(8,128)S(1)} %copy.87, f32[256,128]{0,1:T(8,128)S(1)} %copy.85), kind=kOutput, calls=%fused_computation.94 | convolution fusion | flops 807108608 | bytes 6553600 | tf_op jit(solution)/shard_map/jm,ckm->cjk/dot_general | solution.py:24
  102.8 3.9 %fusion.84 = f32[16,256,128]{2,1,0:T(8,128)S(1)} fusion(f32[16,128,256]{2,1,0:T(8,128)S(1)} %copy-done.2, f32[16,128,256]{2,1,0:T(8,128)S(1)} %copy-done.3, f32[256,128]{0,1:T(8,128)S(1)} %copy.87, f32[256,128]{0,1:T(8,128)S(1)} %copy.85), kind=kOutput, calls=%fused_computation.95 | convolution fusion | flops 807108608 | bytes 6553600 | tf_op jit(solution)/shard_map/jm,ckm->cjk/dot_general | solution.py:24
  106.6 4.1 %fusion.88 = f32[16,256,128]{2,1,0:T(8,128)S(1)} fusion(f32[16,128,256]{2,1,0:T(8,128)S(1)} %copy-done.2, f32[16,128,256]{2,1,0:T(8,128)S(1)} %copy-done.3, f32[256,128]{0,1:T(8,128)S(1)} %copy.87, f32[256,128]{0,1:T(8,128)S(1)} %copy.85), kind=kOutput, calls=%fused_computation.96 | convolution fusion | flops 807108608 | bytes 6553600 | tf_op jit(solution)/shard_map/jm,ckm->cjk/dot_general | solution.py:24
  110.7 3.9 %fusion.72 = f32[16,256,128]{2,1,0:T(8,128)S(1)} fusion(f32[16,128,256]{2,1,0:T(8,128)S(1)} %fusion.101, f32[16,128,256]{2,1,0:T(8,128)S(1)} %copy-done, f32[256,128]{0,1:T(8,128)S(1)} %copy.87, f32[256,128]{0,1:T(8,128)S(1)} %copy.85), kind=kOutput, calls=%fused_computation.91 | convolution fusion | flops 807108608 | bytes 6553600 | tf_op jit(solution)/shard_map/jm,ckm->cjk/dot_general | solution.py:24
  114.6 3.9 %fusion.76 = f32[16,256,128]{2,1,0:T(8,128)S(1)} fusion(f32[16,128,256]{2,1,0:T(8,128)S(1)} %fusion.101, f32[16,128,256]{2,1,0:T(8,128)S(1)} %copy-done, f32[256,128]{0,1:T(8,128)S(1)} %copy.87, f32[256,128]{0,1:T(8,128)S(1)} %copy.85), kind=kOutput, calls=%fused_computation.92 | convolution fusion | flops 807108608 | bytes 6553600 | tf_op jit(solution)/shard_map/jm,ckm->cjk/dot_general | solution.py:24
  118.5 4.4 %convolution_add_fusion.1 = f32[16,256,128]{2,1,0:T(8,128)S(1)} fusion(f32[16,256,128]{2,1,0:T(8,128)S(1)} %fusion.78, f32[16,128,256]{2,1,0:T(8,128)S(1)} %fusion.99, f32[16,128,256]{2,1,0:T(8,128)S(1)} %fusion.108, f32[256,128]{0,1:T(8,128)S(1)} %copy.87, f32[256,128]{0,1:T(8,128)S(1)} %copy.85), kind=kOutput, calls=%fused_computation.54 | convolution fusion | flops 807632896 | bytes 8650752 | tf_op jit(solution)/shard_map/jm,ckm->cjk/dot_general | solution.py:24
  122.9 3.9 %convolution_subtract_fusion.1 = f32[16,256,128]{2,1,0:T(8,128)S(1)} fusion(f32[16,256,128]{2,1,0:T(8,128)S(1)} %fusion.82, f32[16,128,256]{2,1,0:T(8,128)S(1)} %fusion.99, f32[16,128,256]{2,1,0:T(8,128)S(1)} %fusion.108, f32[256,128]{0,1:T(8,128)S(1)} %copy.87, f32[256,128]{0,1:T(8,128)S(1)} %copy.85), kind=kOutput, calls=%fused_computation.56 | convolution fusion | flops 807632896 | bytes 8650752 | tf_op jit(solution)/shard_map/jm,ckm->cjk/dot_general | solution.py:24
  126.8 3.9 %convolution_add_fusion = f32[16,256,128]{2,1,0:T(8,128)S(1)} fusion(f32[16,256,128]{2,1,0:T(8,128)S(1)} %fusion.84, f32[16,128,256]{2,1,0:T(8,128)S(1)} %copy-done.2, f32[16,128,256]{2,1,0:T(8,128)S(1)} %copy-done.3, f32[256,128]{0,1:T(8,128)S(1)} %copy.87, f32[256,128]{0,1:T(8,128)S(1)} %copy.85), kind=kOutput, calls=%fused_computation.52 | convolution fusion | flops 807632896 | bytes 8650752 | tf_op jit(solution)/shard_map/jm,ckm->cjk/dot_general | solution.py:24
  130.8 4.1 %convolution_subtract_fusion = f32[16,256,128]{2,1,0:T(8,128)S(1)} fusion(f32[16,256,128]{2,1,0:T(8,128)S(1)} %fusion.88, f32[16,128,256]{2,1,0:T(8,128)S(1)} %copy-done.2, f32[16,128,256]{2,1,0:T(8,128)S(1)} %copy-done.3, f32[256,128]{0,1:T(8,128)S(1)} %copy.87, f32[256,128]{0,1:T(8,128)S(1)} %copy.85), kind=kOutput, calls=%fused_computation.53 | convolution fusion | flops 807632896 | bytes 8650752 | tf_op jit(solution)/shard_map/jm,ckm->cjk/dot_general | solution.py:24
  134.9 3.9 %convolution_subtract_fusion.2 = f32[16,256,128]{2,1,0:T(8,128)S(1)} fusion(f32[16,256,128]{2,1,0:T(8,128)S(1)} %fusion.76, f32[16,128,256]{2,1,0:T(8,128)S(1)} %fusion.101, f32[16,128,256]{2,1,0:T(8,128)S(1)} %copy-done, f32[256,128]{0,1:T(8,128)S(1)} %copy.87, f32[256,128]{0,1:T(8,128)S(1)} %copy.85), kind=kOutput, calls=%fused_computation.57 | convolution fusion | flops 807632896 | bytes 8650752 | tf_op jit(solution)/shard_map/jm,ckm->cjk/dot_general | solution.py:24
  138.9 6.9 %subtract_subtract_fusion = (f32[16,256,128]{2,1,0:T(8,128)S(1)}, f32[16,256,128]{2,1,0:T(8,128)S(1)}, f32[16,256,128]{2,1,0:T(8,128)}, f32[16,256,128]{2,1,0:T(8,128)}) fusion(f32[16,256,128]{2,1,0:T(8,128)S(1)} %convolution_subtract_fusion, f32[16,256,128]{2,1,0:T(8,128)S(1)} %convolution_subtract_fusion.2, f32[16,256,128]{2,1,0:T(8,128)S(1)} %convolution_add_fusion, ...), kind=kOutput, calls=%fused_computation.37 | convolution fusion | flops 818118656 | bytes 25427968 | tf_op jit(solution)/shard_map/jm,ckm->cjk/dot_general | solution.py:24
  145.8 2.3 fusion
  148.1 2.2 fusion.2
  150.3 2.3 fusion.39
  152.7 2.3 fusion.36
  155.0 2.4 fusion.71
  157.4 2.6 fusion.70
  160.0 3.3 %fusion.56 = bf16[16,128,128]{1,2,0:T(8,128)(2,1)} fusion(f32[16,128,128]{2,1,0:T(8,128)S(1)} %fusion.71, f32[16,256,128]{1,2,0:T(8,128)S(1)} %fusion.39, f32[16,256,128]{1,2,0:T(8,128)S(1)} %fusion.36, f32[256,128]{0,1:T(8,128)S(1)} %copy.87, f32[256,128]{0,1:T(8,128)S(1)} %copy.85), kind=kOutput, calls=%fused_computation.74 | convolution fusion | flops 808124416 | bytes 6029312 | tf_op jit(solution)/shard_map/kn,ckm->cnm/dot_general | solution.py:24
  163.3 2.0 copy.120
  165.3 2.0 convert_element_type.251
  167.3 2.1 copy.121
  169.4 5.9 %all-to-all-start.5 = ((bf16[16,64,256]{2,0,1:T(8,128)(2,1)}), bf16[16,64,256]{2,0,1:T(8,128)(2,1)}, u32[]{:S(2)}, u32[]{:S(2)}) async-start(bf16[16,64,256]{2,0,1:T(8,128)(2,1)} %copy.121), calls=%async_computation.5 | async-start | bytes 1048576 | tf_op jit(solution)/shard_map/all_to_all | solution.py:105
  175.4 4.7 %fusion.55 = bf16[16,128,128]{1,2,0:T(8,128)(2,1)} fusion(f32[16,128,128]{2,1,0:T(8,128)S(1)} %fusion.70, f32[16,256,128]{1,2,0:T(8,128)} %copy-done.1, f32[16,256,128]{1,2,0:T(8,128)S(1)} %fusion.39, f32[256,128]{0,1:T(8,128)S(1)} %copy.87, f32[256,128]{0,1:T(8,128)S(1)} %copy.85), kind=kOutput, calls=%fused_computation.73 | convolution fusion | flops 808124416 | bytes 6029312 | tf_op jit(solution)/shard_map/kn,ckm->cnm/dot_general | solution.py:24
  180.1 1.5 copy.118
  181.7 1.1 copy.119
  182.8 2.3 fusion.10
  185.1 3.6 %fusion.12 = f32[16,256,128]{1,2,0:T(8,128)} fusion(f32[16,256,128]{2,1,0:T(8,128)S(1)} %copy-done.7), kind=kOutput, calls=%fused_computation.16 | convolution fusion | flops 805535744 | bytes 4194304 | tf_op jit(solution)/shard_map/jm,cjk->ckm/dot_general | solution.py:24
  188.7 3.7 %fusion.33 = f32[16,256,128]{1,2,0:T(8,128)} fusion(f32[16,256,128]{1,2,0:T(8,128)S(1)} %fusion.10, f32[16,256,128]{2,1,0:T(8,128)S(1)} %copy-done.4), kind=kOutput, calls=%fused_computation.49 | convolution fusion | flops 806060032 | bytes 6291456 | tf_op jit(solution)/shard_map/jm,cjk->ckm/dot_general | solution.py:24
  192.4 10.5 %all-to-all-start.4 = ((bf16[16,64,256]{2,0,1:T(8,128)(2,1)}), bf16[16,64,256]{2,0,1:T(8,128)(2,1)}, u32[]{:S(2)}, u32[]{:S(2)}) async-start(bf16[16,64,256]{2,0,1:T(8,128)(2,1)} %copy.119), calls=%async_computation.4 | async-start | bytes 1048576 | tf_op jit(solution)/shard_map/all_to_all | solution.py:104
  202.9 4.1 %fusion.30 = f32[16,256,128]{1,2,0:T(8,128)S(1)} fusion(f32[16,256,128]{1,2,0:T(8,128)} %fusion.12, f32[16,256,128]{2,1,0:T(8,128)S(1)} %copy-done.4), kind=kOutput, calls=%fused_computation.48 | convolution fusion | flops 806060032 | bytes 6291456 | tf_op jit(solution)/shard_map/jm,cjk->ckm/dot_general | solution.py:24
  207.0 2.5 fusion.22
  209.5 2.5 fusion.57
  212.5 1.1 copy.105
  213.6 5.5 %all-to-all-done.4 = bf16[16,64,256]{2,0,1:T(8,128)(2,1)} async-done(((bf16[16,64,256]{2,0,1:T(8,128)(2,1)}), bf16[16,64,256]{2,0,1:T(8,128)(2,1)}, u32[]{:S(2)}, u32[]{:S(2)}) %all-to-all-start.4) | async-done | bytes 524320 | tf_op jit(solution)/shard_map/all_to_all | solution.py:104
  219.1 5.9 %all-to-all-start.2 = ((bf16[16,64,256]{2,0,1:T(8,128)(2,1)}), bf16[16,64,256]{2,0,1:T(8,128)(2,1)S(1)}, u32[]{:S(2)}, u32[]{:S(2)}) async-start(bf16[16,64,256]{2,0,1:T(8,128)(2,1)} %copy.105), calls=%async_computation.2 | async-start | bytes 1048576 | tf_op jit(solution)/shard_map/all_to_all | solution.py:93
  225.0 2.0 copy.153
  227.1 14.8 %all-to-all-done.2 = bf16[16,64,256]{2,0,1:T(8,128)(2,1)S(1)} async-done(((bf16[16,64,256]{2,0,1:T(8,128)(2,1)}), bf16[16,64,256]{2,0,1:T(8,128)(2,1)S(1)}, u32[]{:S(2)}, u32[]{:S(2)}) %all-to-all-start.2) | async-done | bytes 524320 | tf_op jit(solution)/shard_map/all_to_all | solution.py:93
  241.9 3.2 %fusion.61 = (bf16[256,1024]{0,1:T(8,128)(2,1)}, bf16[256,1024]{0,1:T(8,128)(2,1)}, bf16[256,1024]{0,1:T(8,128)(2,1)}, bf16[256,1024]{0,1:T(8,128)(2,1)}) fusion(bf16[256,1024]{0,1:T(8,128)(2,1)S(1)} %copy-done.11, bf16[256,1024]{0,1:T(8,128)(2,1)S(1)} %copy-done.17, bf16[16,64,256]{2,0,1:T(8,128)(2,1)} %all-to-all-done.4, f32[1024]{0:T(1024)S(1)} %copy-done.23, ...), kind=kLoop, calls=%fused_computation.77 | loop fusion | flops 5242880 | bytes 6295552 | tf_op jit(solution)/shard_map/convert_element_type | solution.py:117
  245.1 2.1 copy.125
  247.3 2.0 copy.124
  249.3 1.0 copy.122
  250.3 1.0 copy.123
  251.3 18.2 %reduce-scatter.4.cloned.1.call-done = bf16[64,1024]{1,0:T(8,128)(2,1)} async-done(((bf16[256,1024]{1,0:T(8,128)(2,1)}), bf16[64,1024]{1,0:T(8,128)(2,1)}) %reduce-scatter.4.cloned.1.call-update) | async-done | bytes 131088
  269.5 1.1 copy.154
  270.6 0.9 copy.126
  (65 shorter events, 3.1 us)
Async XLA Ops:
  7.2 2.8 %copy-start.20 = (bf16[256,1024]{1,0:T(8,128)(2,1)S(1)}, bf16[256,1024]{1,0:T(8,128)(2,1)}, u32[]{:S(2)}) copy-start(bf16[256,1024]{1,0:T(8,128)(2,1)} %param.8) | copy-start | bytes 1572868
  7.2 3.0 %copy-start.21 = (bf16[256,1024]{1,0:T(8,128)(2,1)S(1)}, bf16[256,1024]{1,0:T(8,128)(2,1)}, u32[]{:S(2)}) copy-start(bf16[256,1024]{1,0:T(8,128)(2,1)} %param.9) | copy-start | bytes 1572868
  8.5 3.0 %copy-start.8 = (bf16[256,1024]{0,1:T(8,128)(2,1)}, bf16[256,1024]{0,1:T(8,128)(2,1)S(1)}, u32[]{:S(2)}) copy-start(bf16[256,1024]{0,1:T(8,128)(2,1)S(1)} %copy.80) | copy-start | bytes 1572868
  10.0 1.5 copy-start.10
  10.2 1.3 copy-start.12
  10.4 30.8 %copy-start.14 = (bf16[256,1024]{0,1:T(8,128)(2,1)}, bf16[256,1024]{0,1:T(8,128)(2,1)S(1)}, u32[]{:S(2)}) copy-start(bf16[256,1024]{0,1:T(8,128)(2,1)S(1)} %copy.106) | copy-start | bytes 1572868
  11.5 29.7 %copy-start.16 = (bf16[256,1024]{0,1:T(8,128)(2,1)}, bf16[256,1024]{0,1:T(8,128)(2,1)S(1)}, u32[]{:S(2)}) copy-start(bf16[256,1024]{0,1:T(8,128)(2,1)S(1)} %get-tuple-element.26) | copy-start | bytes 1572868
  11.5 36.3 %copy-start.22 = (bf16[256,1024]{1,0:T(8,128)(2,1)S(1)}, bf16[256,1024]{1,0:T(8,128)(2,1)}, u32[]{:S(2)}) copy-start(bf16[256,1024]{1,0:T(8,128)(2,1)} %param.10) | copy-start | bytes 1572868
  41.2 22.3 %all-to-all-start = ((bf16[64,16,256]{2,1,0:T(8,128)(2,1)}), bf16[64,16,256]{2,1,0:T(8,128)(2,1)S(1)}, u32[]{:S(2)}, u32[]{:S(2)}) async-start(bf16[64,16,256]{2,1,0:T(8,128)(2,1)} %bitcast.1), calls=%async_computation | async-start | bytes 1048576 | tf_op jit(solution)/shard_map/all_to_all | solution.py:83
  63.6 22.6 %all-to-all-start.1 = ((bf16[64,16,256]{2,1,0:T(8,128)(2,1)}), bf16[64,16,256]{2,1,0:T(8,128)(2,1)}, u32[]{:S(2)}, u32[]{:S(2)}) async-start(bf16[64,16,256]{2,1,0:T(8,128)(2,1)} %bitcast.10), calls=%async_computation.1 | async-start | bytes 1048576 | tf_op jit(solution)/shard_map/all_to_all | solution.py:84
  98.9 3.9 %copy-start.2 = (f32[16,128,256]{2,1,0:T(8,128)S(1)}, f32[16,128,256]{2,1,0:T(8,128)}, u32[]{:S(2)}) copy-start(f32[16,128,256]{2,1,0:T(8,128)} %fusion.96) | copy-start | bytes 6291460
  98.9 3.9 %copy-start.3 = (f32[16,128,256]{2,1,0:T(8,128)S(1)}, f32[16,128,256]{2,1,0:T(8,128)}, u32[]{:S(2)}) copy-start(f32[16,128,256]{2,1,0:T(8,128)} %fusion.105) | copy-start | bytes 6291460
  106.6 4.1 %copy-start = (f32[16,128,256]{2,1,0:T(8,128)S(1)}, f32[16,128,256]{2,1,0:T(8,128)}, u32[]{:S(2)}) copy-start(f32[16,128,256]{2,1,0:T(8,128)} %fusion.110) | copy-start | bytes 6291460
  155.0 5.1 %copy-start.1 = (f32[16,256,128]{1,2,0:T(8,128)}, f32[16,256,128]{1,2,0:T(8,128)S(1)}, u32[]{:S(2)}) copy-start(f32[16,256,128]{1,2,0:T(8,128)S(1)} %fusion.36) | copy-start | bytes 6291460
  169.4 23.0 %all-to-all-start.5 = ((bf16[16,64,256]{2,0,1:T(8,128)(2,1)}), bf16[16,64,256]{2,0,1:T(8,128)(2,1)}, u32[]{:S(2)}, u32[]{:S(2)}) async-start(bf16[16,64,256]{2,0,1:T(8,128)(2,1)} %copy.121), calls=%async_computation.5 | async-start | bytes 1048576 | tf_op jit(solution)/shard_map/all_to_all | solution.py:105
  180.1 2.7 copy-start.6
  182.8 2.3 copy-start.7
  185.1 3.6 %copy-start.4 = (f32[16,256,128]{2,1,0:T(8,128)S(1)}, f32[16,256,128]{2,1,0:T(8,128)}, u32[]{:S(2)}) copy-start(f32[16,256,128]{2,1,0:T(8,128)} %get-tuple-element.18) | copy-start | bytes 6291460
  192.4 26.7 %all-to-all-start.4 = ((bf16[16,64,256]{2,0,1:T(8,128)(2,1)}), bf16[16,64,256]{2,0,1:T(8,128)(2,1)}, u32[]{:S(2)}, u32[]{:S(2)}) async-start(bf16[16,64,256]{2,0,1:T(8,128)(2,1)} %copy.119), calls=%async_computation.4 | async-start | bytes 1048576 | tf_op jit(solution)/shard_map/all_to_all | solution.py:104
  202.9 4.1 %copy-start.5 = (f32[16,256,128]{1,2,0:T(8,128)S(1)}, f32[16,256,128]{1,2,0:T(8,128)}, u32[]{:S(2)}) copy-start(f32[16,256,128]{1,2,0:T(8,128)} %fusion.33) | copy-start | bytes 6291460
  212.5 29.4 %copy-start.9 = (bf16[256,1024]{0,1:T(8,128)(2,1)S(1)}, bf16[256,1024]{0,1:T(8,128)(2,1)}, u32[]{:S(2)}) copy-start(bf16[256,1024]{0,1:T(8,128)(2,1)} %copy-done.8) | copy-start | bytes 1572868
  212.5 29.4 %copy-start.11 = (bf16[256,1024]{0,1:T(8,128)(2,1)S(1)}, bf16[256,1024]{0,1:T(8,128)(2,1)}, u32[]{:S(2)}) copy-start(bf16[256,1024]{0,1:T(8,128)(2,1)} %copy-done.10) | copy-start | bytes 1572868
  212.5 29.4 %copy-start.13 = (bf16[256,1024]{0,1:T(8,128)(2,1)S(1)}, bf16[256,1024]{0,1:T(8,128)(2,1)}, u32[]{:S(2)}) copy-start(bf16[256,1024]{0,1:T(8,128)(2,1)} %copy-done.12) | copy-start | bytes 1572868
  212.5 29.4 %copy-start.15 = (bf16[256,1024]{0,1:T(8,128)(2,1)S(1)}, bf16[256,1024]{0,1:T(8,128)(2,1)}, u32[]{:S(2)}) copy-start(bf16[256,1024]{0,1:T(8,128)(2,1)} %copy-done.14) | copy-start | bytes 1572868
  212.5 29.4 %copy-start.17 = (bf16[256,1024]{0,1:T(8,128)(2,1)S(1)}, bf16[256,1024]{0,1:T(8,128)(2,1)}, u32[]{:S(2)}) copy-start(bf16[256,1024]{0,1:T(8,128)(2,1)} %copy-done.16) | copy-start | bytes 1572868
  212.5 29.4 %copy-start.23 = (f32[1024]{0:T(1024)S(1)}, f32[1024]{0:T(1024)}, u32[]{:S(2)}) copy-start(f32[1024]{0:T(1024)} %param.11) | copy-start | bytes 12292
  219.1 22.8 %all-to-all-start.2 = ((bf16[16,64,256]{2,0,1:T(8,128)(2,1)}), bf16[16,64,256]{2,0,1:T(8,128)(2,1)S(1)}, u32[]{:S(2)}, u32[]{:S(2)}) async-start(bf16[16,64,256]{2,0,1:T(8,128)(2,1)} %copy.105), calls=%async_computation.2 | async-start | bytes 1048576 | tf_op jit(solution)/shard_map/all_to_all | solution.py:93
  225.0 44.5 %reduce-scatter.4.cloned.1.call-start = ((), (), s32[]{:S(2)}) async-start(), calls=%async_computation.7 | async-start | bytes 655360
  245.1 4.2 %copy-start.19 = (bf16[256,1024]{0,1:T(8,128)(2,1)S(1)}, bf16[256,1024]{0,1:T(8,128)(2,1)}, u32[]{:S(2)}) copy-start(bf16[256,1024]{0,1:T(8,128)(2,1)} %get-tuple-element.23) | copy-start | bytes 1572868
  245.1 5.2 %copy-start.18 = (bf16[256,1024]{0,1:T(8,128)(2,1)S(1)}, bf16[256,1024]{0,1:T(8,128)(2,1)}, u32[]{:S(2)}) copy-start(bf16[256,1024]{0,1:T(8,128)(2,1)} %get-tuple-element.24) | copy-start | bytes 1572868
Sparse Core Ops, SparseCore 0:
  228.6 40.8 reduce-scatter.3
where the time goes:
time: 284 us; the launch traced here: 279 us
  matrix products  106 us (37%)
  waiting for transfers between devices  58.7 us (21%)
  starting transfers between devices  34 us (12%)
  blocking collectives  29.7 us (10%)
  local copies, waits for them, and re-layouts  28.6 us (10%)
  between operations  14.9 us (5%)
  other arithmetic  6.49 us (2%)
    dot_general x32, matrix products, contract(): jnp.einsum(form, table, operand, precision=lax.Precision.HIGHEST, preferr...  106 us
    all_to_all x1, blocking collectives, shards(): lax.all_to_all(grad_in.T, 'context', split_axis=0, concat_axis=1, tiled=T...  29.7 us
    unnamed x2, waiting for transfers between devices  18.2 us
    all_to_all x1, waiting for transfers between devices, shards(): lax.all_to_all(conv, 'context', split_axis=1, concat_axis=0, tiled=True)  14.8 us
    unnamed x60, local copies, waits for them, and re-layouts  14.4 us
    all_to_all x1, waiting for transfers between devices, shards(): lax.all_to_all(gated.T, 'context', split_axis=0, concat_axis=1, tiled=True)  14.4 us
    all_to_all x1, starting transfers between devices, shards(): lax.all_to_all(back, 'context', split_axis=1, concat_axis=0, tiled=True)  10.5 us
    all_to_all x1, starting transfers between devices, shards(): lax.all_to_all(filter_param.T, 'context', split_axis=0, concat_axis=1, ti...  6.33 us
  transfers between devices with their start and end apart: 6, of which 5 were waited for; matrix products, arithmetic and copies ran while one was open for 19% of the time, Pallas kernels for 0%

commit v1 on v0

v1 whole, which is shorter than its diff:
```python
import functools
import math

import jax
import jax.numpy as jnp
import ml_dtypes
import numpy as np
from jax import lax
from jax.experimental import pallas as pl
from jax.experimental.pallas import tpu as pltpu
from jax.sharding import PartitionSpec as P

MESH = pl.DeviceIdType.MESH
F32 = jnp.float32
BF16 = jnp.bfloat16


def make_tables(blocks, span):
    length = blocks * span
    row = np.arange(blocks, dtype=np.float64)
    col = np.arange(span, dtype=np.float64)
    outer = 2.0 * np.pi * np.outer(row + 0.25, row) / blocks
    twist = 2.0 * np.pi * np.outer(row + 0.25, col) / length
    inner = 2.0 * np.pi * (np.outer(col, col) % span) / span
    outer_fwd = np.concatenate([np.cos(outer), -np.sin(outer)], axis=0)
    outer_inv = np.concatenate([np.cos(outer).T, -np.sin(outer).T], axis=1)
    cos, sin = np.cos(inner), np.sin(inner)
    inner_fwd = np.block([[cos, -sin], [sin, cos]])
    inner_inv = np.block([[cos, sin], [-sin, cos]])
    half = ml_dtypes.bfloat16
    return (
        outer_fwd.astype(half),
        outer_inv.astype(half),
        np.cos(twist).astype(np.float32),
        (-np.sin(twist)).astype(np.float32),
        inner_fwd.astype(half),
        inner_inv.astype(half),
    )


def dot(a, b):
    return jnp.dot(a, b, preferred_element_type=F32)


def spread(turned, groups):
    rows, span = turned.shape
    part = rows // (2 * groups)
    first = turned[: rows // 2].reshape(groups, part, span)
    second = turned[rows // 2 :].reshape(groups, part, span)
    return jnp.concatenate([first, second], axis=1).astype(BF16)


def gather_rows(blocks):
    groups, rows, span = blocks.shape
    wide = blocks.astype(F32)
    first = wide[:, : rows // 2].reshape(groups * rows // 2, span)
    second = wide[:, rows // 2 :].reshape(groups * rows // 2, span)
    return jnp.concatenate([first, second], axis=0)


def fold(rows):
    half = rows.shape[2] // 2
    return jnp.concatenate([rows[:, :, :half], rows[:, :, half:]], axis=1).astype(BF16)


def unfold(rows):
    part = rows.shape[1] // 2
    wide = rows.astype(F32)
    return jnp.concatenate([wide[:, :part], wide[:, part:]], axis=2)


def kernel(
    groups,
    scale,
    q_ref, k_ref, v_ref, g_ref, f_ref, skip_ref,
    outer_fwd, outer_inv, twist_cos, twist_sin, inner_fwd, inner_inv,
    out_ref, dq_ref, dk_ref, dv_ref, df_ref,
    x_send, x_recv, g_send, g_recv, c_send, c_recv, b_send, b_recv,
    f_send, f_recv, f_other, r_mine, r_other, r_send, r_recv,
    h_send, h_recv, t_send, t_recv,
    time_buf, spec_x, spec_h, spec_g,
    send_sem, recv_sem,
):
    span = q_ref.shape[0]
    chans = x_send.shape[1]
    step = min(4, chans)
    me = lax.axis_index("context")
    mine = lax.axis_index("tensor")
    core = mine % 2
    upper = mine // 2
    sibling = mine + 1 - 2 * core
    across = mine + 2 - 4 * upper

    def start_all(src, dst, slot):
        def body(s, carry):
            to = (me + s) % groups
            pltpu.make_async_remote_copy(
                src_ref=src.at[to], dst_ref=dst.at[me],
                send_sem=send_sem.at[slot], recv_sem=recv_sem.at[slot],
                device_id={"context": to}, device_id_type=MESH,
            ).start()
            return carry
        lax.fori_loop(1, groups, body, 0)
        dst[pl.ds(me, 1)] = src[pl.ds(me, 1)]

    def all_of(src, dst, slot):
        return pltpu.make_async_remote_copy(
            src_ref=src.at[pl.ds(0, groups - 1)], dst_ref=dst.at[pl.ds(0, groups - 1)],
            send_sem=send_sem.at[slot], recv_sem=recv_sem.at[slot],
            device_id={"context": (me + 1) % groups}, device_id_type=MESH,
        )

    def one(src, dst, slot, to):
        return pltpu.make_async_remote_copy(
            src_ref=src, dst_ref=dst,
            send_sem=send_sem.at[slot], recv_sem=recv_sem.at[slot],
            device_id={"tensor": to}, device_id_type=MESH,
        )

    def fill(field):
        flat = field.reshape(groups * chans, span)
        time_buf[0] = flat[:, : span // 2]
        time_buf[1] = flat[:, span // 2 :]

    def filled():
        flat = jnp.concatenate([time_buf[0], time_buf[1]], axis=1)
        return flat.reshape(groups, chans, span)

    def forward(dst):
        def body(n, carry):
            parts = []
            for c in range(step):
                rows = pl.ds(n * step + c, groups, stride=chans)
                field = jnp.concatenate([time_buf[0, rows, :], time_buf[1, rows, :]], axis=1)
                field = field.astype(BF16)
                first = dot(outer_fwd[...], field)
                re, im = first[:groups], first[groups:]
                tc, ts = twist_cos[...], twist_sin[...]
                parts.append(
                    jnp.concatenate([re * tc - im * ts, re * ts + im * tc], axis=1).astype(BF16)
                )
            rows = jnp.concatenate(parts, axis=0)
            dst[pl.ds(pl.multiple_of(n * step * groups, step * groups), step * groups), :] = dot(
                rows, inner_fwd[...]
            )
            return carry
        lax.fori_loop(0, chans // step, body, 0)

    def inverse(a_ref, b_ref, conj):
        def body(n, carry):
            here = pl.ds(pl.multiple_of(n * step * groups, step * groups), step * groups)
            ar, ai = a_ref[here, :span], a_ref[here, span:]
            br, bi = b_ref[here, :span], b_ref[here, span:]
            if conj:
                re, im = ar * br + ai * bi, ar * bi - ai * br
            else:
                re, im = ar * br - ai * bi, ar * bi + ai * br
            prod = jnp.concatenate([re, im], axis=1).astype(BF16)
            back = dot(prod, inner_inv[...])
            tc, ts = twist_cos[...], twist_sin[...]
            for c in range(step):
                re = back[c * groups : (c + 1) * groups, :span]
                im = back[c * groups : (c + 1) * groups, span:]
                both = jnp.concatenate([re * tc + im * ts, im * tc - re * ts], axis=0)
                field = dot(outer_inv[...], both.astype(BF16)) * scale
                rows = pl.ds(n * step + c, groups, stride=chans)
                time_buf[0, rows, :] = field[:, : span // 2]
                time_buf[1, rows, :] = field[:, span // 2 :]
            return carry
        lax.fori_loop(0, chans // step, body, 0)

    def product(a_ref, b_ref):
        return (a_ref[...].astype(F32) * b_ref[...].astype(F32)).astype(BF16).astype(F32)

    first_core = core == 0

    width = f_ref.shape[1]
    taps = f_ref[...].astype(F32)
    taps = jnp.where(first_core, taps[:, : width // 2], taps[:, width // 2 :]).T
    f_send[...] = fold(taps.reshape(groups, chans // 2, span))
    start_all(f_send, f_recv, 0)
    x_send[...] = spread(product(k_ref, v_ref).T, groups)
    start_all(x_send, x_recv, 1)
    g_send[...] = spread(product(q_ref, g_ref).T, groups)
    start_all(g_send, g_recv, 2)

    all_of(f_send, f_recv, 0).wait()
    swap = one(f_recv, f_other, 3, sibling)
    swap.start()
    swap.wait()
    held, other = unfold(f_recv[...]), unfold(f_other[...])
    taps = jnp.concatenate(
        [jnp.where(first_core, held, other), jnp.where(first_core, other, held)], axis=1
    )
    fill(taps)
    forward(spec_h)

    all_of(x_send, x_recv, 1).wait()
    fill(x_recv[...].astype(F32))
    forward(spec_x)
    inverse(spec_x, spec_h, False)
    c_send[...] = filled().astype(BF16)
    start_all(c_send, c_recv, 4)

    all_of(g_send, g_recv, 2).wait()
    fill(g_recv[...].astype(F32))
    forward(spec_g)
    inverse(spec_x, spec_g, True)
    corr = filled()
    low, high = corr[:, : chans // 2], corr[:, chans // 2 :]
    r_mine[...] = fold(jnp.where(first_core, high, low))
    swap = one(r_mine, r_other, 5, sibling)
    swap.start()
    kept = jnp.where(first_core, low, high)
    swap.wait()
    r_send[...] = fold(kept + unfold(r_other[...]))
    start_all(r_send, r_recv, 6)

    inverse(spec_h, spec_g, True)
    b_send[...] = filled().astype(BF16)
    start_all(b_send, b_recv, 7)

    skip = skip_ref[...]
    all_of(c_send, c_recv, 4).wait()
    mixed = gather_rows(c_recv[...]).T + skip * product(k_ref, v_ref)
    out_ref[...] = (q_ref[...].astype(F32) * mixed).astype(BF16)
    dq_ref[...] = (g_ref[...].astype(F32) * mixed).astype(BF16)

    all_of(r_send, r_recv, 6).wait()
    part = r_recv[...].astype(F32)
    rows = groups * chans // 2
    low = part[:, : chans // 2].reshape(rows, span // 2)
    high = part[:, chans // 2 :].reshape(rows, span // 2)
    h_send[...] = jnp.where(upper == 0, high, low).astype(BF16)
    swap = one(h_send, h_recv, 8, across)
    swap.start()

    all_of(b_send, b_recv, 7).wait()
    turned = gather_rows(b_recv[...]).T + skip * product(q_ref, g_ref)
    dk_ref[...] = (turned * v_ref[...].astype(F32)).astype(BF16)
    dv_ref[...] = (turned * k_ref[...].astype(F32)).astype(BF16)

    swap.wait()
    total = (jnp.where(upper == 0, low, high) + h_recv[...].astype(F32)).T
    quarter = span // 4
    t_send[...] = jnp.where(first_core, total[quarter:], total[:quarter])
    swap = one(t_send, t_recv, 9, sibling)
    swap.start()
    held = jnp.where(first_core, total[:quarter], total[quarter:])
    swap.wait()
    other = t_recv[...]
    df_ref[:, : width // 2] = jnp.where(first_core, held, other)
    df_ref[:, width // 2 :] = jnp.where(first_core, other, held)


def shards(queries, keys, values, cotangent, filter_param, skip):
    span, width = queries.shape
    groups = lax.axis_size("context")
    chans = width // groups
    length = groups * span
    scale = 1.0 / (length * math.sqrt(length))
    tables = make_tables(groups, span)
    whole = pl.BlockSpec(memory_space=pltpu.VMEM)
    big = pltpu.VMEM((groups, chans, span), BF16)
    small = pltpu.VMEM((groups, chans, span // 2), BF16)
    wide = jax.ShapeDtypeStruct((span, width), BF16)
    return pl.pallas_call(
        functools.partial(kernel, groups, scale),
        out_shape=(wide, wide, wide, wide, jax.ShapeDtypeStruct((span // 4, width), F32)),
        in_specs=[whole] * 12,
        out_specs=(whole,) * 5,
        scratch_shapes=[big] * 8
        + [small] * 7
        + [pltpu.VMEM((groups * chans // 2, span // 2), BF16)] * 2
        + [pltpu.VMEM((span // 4, width // 2), F32)] * 2
        + [pltpu.VMEM((2, groups * chans, span // 2), F32)]
        + [pltpu.VMEM((groups * chans, 2 * span), F32)] * 3
        + [pltpu.SemaphoreType.DMA((10,))] * 2,
        compiler_params=pltpu.CompilerParams(
            has_side_effects=True, vmem_limit_bytes=56 * 1024 * 1024
        ),
    )(queries, keys, values, cotangent, filter_param, skip.reshape(1, width), *tables)


def solution(mesh):
    placed = (
        P("context", "tensor"),
        P("context", "tensor"),
        P("context", "tensor"),
        P("context", "tensor"),
        P("context", None),
        P("tensor"),
    )
    return jax.shard_map(
        shards,
        mesh=mesh,
        in_specs=placed,
        out_specs=(
            P("context", "tensor"),
            P("context", "tensor"),
            P("context", "tensor"),
            P("context", "tensor"),
            P(("context", "tensor"), None),
        ),
        check_vma=False,
    )
```

time: 284 us -> 93.5 us (0.33); the launches traced: 279 us -> 93 us
  matrix products: 106 us -> 0 us
  Pallas kernels: 0 us -> 86.2 us
  waiting for transfers between devices: 58.7 us -> 0 us
  starting transfers between devices: 34 us -> 0 us
  blocking collectives: 29.7 us -> 0 us
  local copies, waits for them, and re-layouts: 28.6 us -> 6.18 us
  between operations: 14.9 us -> 0.65 us
  other arithmetic: 6.49 us -> 0 us
    dot_general x32 -> x0, matrix products: 106 us -> none  [contract(): jnp.einsum(form, table, operand, precision=lax.Precision.HIGHEST, preferr...]
    pallas_call x0 -> x1, Pallas kernels: none -> 86.2 us  [shards(): pl.pallas_call(functools.partial(kernel, groups, scale), out_shape=(wide,...]
    all_to_all x5 -> x0, waiting for transfers between devices: 40.5 us -> none  [the longest x1 14.8 us: shards(): lax.all_to_all(conv, 'context', split_axis=1, concat_axis=0, tiled=True)]
    all_to_all x5 -> x0, starting transfers between devices: 33.9 us -> none  [the longest x1 10.5 us: shards(): lax.all_to_all(back, 'context', split_axis=1, concat_axis=0, tiled=True)]
    all_to_all x1 -> x0, blocking collectives: 29.7 us -> none  [shards(): lax.all_to_all(grad_in.T, 'context', split_axis=0, concat_axis=1, tiled=T...]
    unnamed x2 -> x0, waiting for transfers between devices: 18.2 us -> none
    convert_element_type x9 -> x0, local copies, waits for them, and re-layouts: 10.4 us -> none  [the longest x3 6.16 us: shards(): corr.astype(jnp.bfloat16)]
    unnamed x60 -> x13, local copies, waits for them, and re-layouts: 14.4 us -> 6.18 us
  transfers between devices with their start and end apart: 6 -> 0, of which waited for: 5 -> 0; matrix products, arithmetic and copies ran while one was open for 19% -> 0% of each run, Pallas kernels for 0% -> 0%
where the time goes in v1:
time: 93.5 us; the launch traced here: 93 us
  Pallas kernels  86.2 us (92%)
  local copies, waits for them, and re-layouts  6.18 us (7%)
    pallas_call x1, Pallas kernels, shards(): pl.pallas_call(functools.partial(kernel, groups, scale), out_shape=(wide,...  86.2 us
    unnamed x13, local copies, waits for them, and re-layouts  6.18 us

profile of v1, /device:TPU:1, one launch (start us, length us, event | category | flops | bytes accessed | tf_op | source)
XLA Modules:
  0.0 93.0 jit_solution(17233534126220379853)
XLA Ops:
  0.6 86.2 %shard_map.155 = (bf16[256,1024]{1,0:T(8,128)(2,1)}, bf16[256,1024]{1,0:T(8,128)(2,1)}, bf16[256,1024]{1,0:T(8,128)(2,1)}, bf16[256,1024]{1,0:T(8,128)(2,1)}, f32[64,1024]{1,0:T(8,128)}) custom-call(bf16[256,1024]{1,0:T(8,128)(2,1)} %q_ref.1, bf16[256,1024]{1,0:T(8,128)(2,1)} %k_ref.1, bf16[256,1024]{1,0:T(8,128)(2,1)} %v_ref.1, bf16[256,1024]{1,0:T(8,128)(2,1)} %g_ref.1, ...), custom_call_target="tpu_custom_call" | custom-call | tf_op jit(solution)/shard_map/pallas_call | solution.py:267
  86.8 0.0 copy-start.2
  86.8 1.9 %copy.22 = bf16[256,1024]{1,0:T(8,128)(2,1)} copy(bf16[256,1024]{1,0:T(8,128)(2,1)} %get-tuple-element.10) | data formatting | bytes 1048576
  88.8 0.0 copy-done.2
  88.8 0.0 copy-start.1
  88.8 0.8 copy.23
  89.6 0.4 copy-done.1
  90.0 0.0 copy-start
  90.0 0.8 copy.24
  90.8 0.4 copy-done
  91.2 0.0 copy-start.3
  91.2 0.8 copy.25
  92.0 0.3 copy-done.3
  92.3 0.7 copy.26
Async XLA Ops:
  86.8 1.9 %copy-start.2 = (bf16[256,1024]{1,0:T(8,128)(2,1)S(1)}, bf16[256,1024]{1,0:T(8,128)(2,1)}, u32[]{:S(2)}) copy-start(bf16[256,1024]{1,0:T(8,128)(2,1)} %get-tuple-element.11) | copy-start | bytes 1572868
  88.8 1.2 %copy-start.1 = (bf16[256,1024]{1,0:T(8,128)(2,1)S(1)}, bf16[256,1024]{1,0:T(8,128)(2,1)}, u32[]{:S(2)}) copy-start(bf16[256,1024]{1,0:T(8,128)(2,1)} %get-tuple-element.12) | copy-start | bytes 1572868
  90.0 1.2 %copy-start = (bf16[256,1024]{1,0:T(8,128)(2,1)S(1)}, bf16[256,1024]{1,0:T(8,128)(2,1)}, u32[]{:S(2)}) copy-start(bf16[256,1024]{1,0:T(8,128)(2,1)} %get-tuple-element.13) | copy-start | bytes 1572868
  91.2 1.1 %copy-start.3 = (f32[64,1024]{1,0:T(8,128)S(1)}, f32[64,1024]{1,0:T(8,128)}, u32[]{:S(2)}) copy-start(f32[64,1024]{1,0:T(8,128)} %get-tuple-element.14) | copy-start | bytes 786436

commit v2 on v1

v2 whole, which is shorter than its diff:
```python
import functools
import math

import jax
import jax.numpy as jnp
import ml_dtypes
import numpy as np
from jax import lax
from jax.experimental import pallas as pl
from jax.experimental.pallas import tpu as pltpu
from jax.sharding import PartitionSpec as P

MESH = pl.DeviceIdType.MESH
F32 = jnp.float32
BF16 = jnp.bfloat16


def make_tables(blocks, span):
    length = blocks * span
    row = np.arange(blocks, dtype=np.float64)
    col = np.arange(span, dtype=np.float64)
    outer = 2.0 * np.pi * np.outer(row + 0.25, row) / blocks
    twist = 2.0 * np.pi * np.outer(row + 0.25, col) / length
    inner = 2.0 * np.pi * (np.outer(col, col) % span) / span
    outer_fwd = np.concatenate([np.cos(outer), -np.sin(outer)], axis=0)
    outer_inv = np.concatenate([np.cos(outer).T, -np.sin(outer).T], axis=1)
    cos, sin = np.cos(inner), np.sin(inner)
    inner_fwd = np.block([[cos, -sin], [sin, cos]])
    inner_inv = np.block([[cos, sin], [-sin, cos]])
    half = ml_dtypes.bfloat16
    return (
        outer_fwd.astype(half),
        outer_inv.astype(half),
        np.cos(twist).astype(np.float32),
        (-np.sin(twist)).astype(np.float32),
        inner_fwd.astype(half),
        inner_inv.astype(half),
    )


def dot(a, b):
    return jnp.dot(a, b, preferred_element_type=F32)


def spread(turned, groups):
    rows, span = turned.shape
    part = rows // (2 * groups)
    first = turned[: rows // 2].reshape(groups, part, span)
    second = turned[rows // 2 :].reshape(groups, part, span)
    return jnp.concatenate([first, second], axis=1).astype(BF16)


def gather_rows(blocks):
    groups, rows, span = blocks.shape
    wide = blocks.astype(F32)
    first = wide[:, : rows // 2].reshape(groups * rows // 2, span)
    second = wide[:, rows // 2 :].reshape(groups * rows // 2, span)
    return jnp.concatenate([first, second], axis=0)


def fold(rows):
    half = rows.shape[2] // 2
    return jnp.concatenate([rows[:, :, :half], rows[:, :, half:]], axis=1).astype(BF16)


def unfold(rows):
    part = rows.shape[1] // 2
    wide = rows.astype(F32)
    return jnp.concatenate([wide[:, :part], wide[:, part:]], axis=2)


def kernel(
    groups,
    side,
    scale,
    q_hbm, k_hbm, v_hbm, g_hbm, f_hbm,
    outer_fwd_hbm, outer_inv_hbm, twist_cos_hbm, twist_sin_hbm, inner_fwd_hbm, inner_inv_hbm,
    conv_ref, back_ref, df_ref,
    q_ref, k_ref, v_ref, g_ref, f_ref,
    outer_fwd, outer_inv, twist_cos, twist_sin, inner_fwd, inner_inv,
    x_send, x_recv, g_send, g_recv, c_send, c_recv, b_send, b_recv,
    f_send, f_recv, f_other, r_mine, r_other,
    r_send, r_mid, s_send, s_recv, t_send, t_recv,
    time_buf, spec_x, spec_h, spec_g,
    load_sem, send_sem, recv_sem, ring_sem, line_sem,
):
    span, width = q_ref.shape
    chans = x_send.shape[1]
    part = chans // 2
    ring = 2 * side
    step = min(4, chans)
    me = lax.axis_index("context")
    mine = lax.axis_index("tensor")
    core = mine % 2
    upper = mine // 2
    sibling = mine + 1 - 2 * core
    mx, mz, my = me // (side * side), (me // side) % side, me % side
    plane = upper * side + mz
    place = mx * side + my
    near = (mz // (side // 2) + upper) % 2
    first_core = core == 0

    def at_place(s):
        x, y = s // side, s % side
        return {"context": (x * side + mz) * side + y}

    def at_plane(p):
        return {"context": (mx * side + p % side) * side + my, "tensor": (p // side) * 2 + core}

    def along_x(s):
        return {"context": (((mx + s) % side) * side + mz) * side + my}

    def along_y(s):
        return {"context": (mx * side + mz) * side + (my + s) % side}

    def along_ring(s):
        return at_plane((plane + s) % ring)

    def greet(sem, where, count):
        def body(s, carry):
            pl.semaphore_signal(sem, inc=1, device_id=where(s), device_id_type=MESH)
            return carry
        lax.fori_loop(1, count, body, 0)

    def remote(src, dst, slot, where):
        return pltpu.make_async_remote_copy(
            src_ref=src, dst_ref=dst,
            send_sem=send_sem.at[slot], recv_sem=recv_sem.at[slot],
            device_id=where, device_id_type=MESH,
        )

    def start_all(src, dst, slot):
        def body(s, carry):
            to = (me + s) % groups
            remote(src.at[to], dst.at[me], slot, {"context": to}).start()
            return carry
        lax.fori_loop(1, groups, body, 0)
        dst[pl.ds(me, 1)] = src[pl.ds(me, 1)]

    def start_nearest(src, dst, slot):
        def body(s, carry):
            to = (me + s) % groups
            up = (near + ((to // side) % side) // (side // 2)) % 2
            remote(src.at[to], dst.at[me], slot, {"context": to, "tensor": 2 * up + core}).start()
            return carry
        lax.fori_loop(1, groups, body, 0)
        dst[pl.ds(me, 1)] = src[pl.ds(me, 1)]

    def start_plane(src, dst, slot):
        def body(s, carry):
            to = (place + s) % (side * side)
            remote(src.at[to // side, :, to % side], dst.at[place], slot, at_place(to)).start()
            return carry
        lax.fori_loop(1, side * side, body, 0)
        dst[pl.ds(place, 1)] = src[pl.ds(mx, 1), :, my]

    def start_ring(src, dst, slot):
        def body(s, carry):
            to = (plane + s) % ring
            remote(src.at[to], dst.at[plane], slot, at_plane(to)).start()
            return carry
        lax.fori_loop(1, ring, body, 0)
        dst[pl.ds(plane, 1)] = src[pl.ds(plane, 1)]

    def wait_all(dst, slot):
        blocks = dst.at[pl.ds(0, dst.shape[0] - 1)]
        remote(blocks, blocks, slot, {"tensor": sibling}).wait()

    def fill(field):
        flat = field.reshape(groups * chans, span)
        time_buf[0] = flat[:, : span // 2]
        time_buf[1] = flat[:, span // 2 :]

    def filled():
        flat = jnp.concatenate([time_buf[0], time_buf[1]], axis=1)
        return flat.reshape(groups, chans, span)

    def forward(dst):
        def body(n, carry):
            parts = []
            for c in range(step):
                rows = pl.ds(n * step + c, groups, stride=chans)
                field = jnp.concatenate([time_buf[0, rows, :], time_buf[1, rows, :]], axis=1)
                first = dot(outer_fwd[...], field.astype(BF16))
                re, im = first[:groups], first[groups:]
                tc, ts = twist_cos[...], twist_sin[...]
                parts.append(
                    jnp.concatenate([re * tc - im * ts, re * ts + im * tc], axis=1).astype(BF16)
                )
            rows = jnp.concatenate(parts, axis=0)
            here = pl.ds(pl.multiple_of(n * step * groups, step * groups), step * groups)
            dst[here, :] = dot(rows, inner_fwd[...])
            return carry
        lax.fori_loop(0, chans // step, body, 0)

    def inverse(a_ref, b_ref, conj):
        def body(n, carry):
            here = pl.ds(pl.multiple_of(n * step * groups, step * groups), step * groups)
            ar, ai = a_ref[here, :span], a_ref[here, span:]
            br, bi = b_ref[here, :span], b_ref[here, span:]
            if conj:
                re, im = ar * br + ai * bi, ar * bi - ai * br
            else:
                re, im = ar * br - ai * bi, ar * bi + ai * br
            prod = jnp.concatenate([re, im], axis=1).astype(BF16)
            back = dot(prod, inner_inv[...])
            tc, ts = twist_cos[...], twist_sin[...]
            for c in range(step):
                re = back[c * groups : (c + 1) * groups, :span]
                im = back[c * groups : (c + 1) * groups, span:]
                both = jnp.concatenate([re * tc + im * ts, im * tc - re * ts], axis=0)
                field = dot(outer_inv[...], both.astype(BF16)) * scale
                rows = pl.ds(n * step + c, groups, stride=chans)
                time_buf[0, rows, :] = field[:, : span // 2]
                time_buf[1, rows, :] = field[:, span // 2 :]
            return carry
        lax.fori_loop(0, chans // step, body, 0)

    def product(a_ref, b_ref):
        return (a_ref[...].astype(F32) * b_ref[...].astype(F32)).astype(BF16).astype(F32)

    loads = [
        pltpu.make_async_copy(src, dst, load_sem.at[n])
        for n, (src, dst) in enumerate(
            [
                (k_hbm, k_ref), (v_hbm, v_ref), (f_hbm, f_ref), (q_hbm, q_ref), (g_hbm, g_ref),
                (outer_fwd_hbm, outer_fwd), (twist_cos_hbm, twist_cos), (twist_sin_hbm, twist_sin),
                (inner_fwd_hbm, inner_fwd), (inner_inv_hbm, inner_inv), (outer_inv_hbm, outer_inv),
            ]
        )
    ]
    for load in loads:
        load.start()

    barrier = pltpu.get_barrier_semaphore()
    greet(barrier, along_x, side)
    greet(barrier, along_y, side)
    greet(barrier, along_ring, ring)
    pl.semaphore_signal(barrier, inc=1, device_id={"tensor": sibling}, device_id_type=MESH)
    loads[0].wait()
    loads[1].wait()
    x_send[...] = spread(product(k_ref, v_ref).T, groups)
    pl.semaphore_wait(barrier, 2 * side + ring - 2)
    greet(ring_sem, along_ring, ring)
    loads[2].wait()
    taps = f_ref[...].astype(F32)
    taps = jnp.where(first_core, taps[:, : width // 2], taps[:, width // 2 :]).T
    f_send[...] = fold(taps.reshape(groups, part, span))
    pl.semaphore_wait(ring_sem, ring - 1)
    greet(line_sem, along_x, side)
    pl.semaphore_wait(line_sem, side - 1)

    start_all(x_send, x_recv, 0)
    start_nearest(f_send, f_recv, 1)
    loads[3].wait()
    loads[4].wait()
    g_send[...] = spread(product(q_ref, g_ref).T, groups)
    start_all(g_send, g_recv, 2)
    for load in loads[5:]:
        load.wait()

    wait_all(f_recv, 1)
    swap = remote(f_recv, f_other, 3, {"tensor": sibling})
    swap.start()
    swap.wait()
    held, other = unfold(f_recv[...]), unfold(f_other[...])
    fill(
        jnp.concatenate(
            [jnp.where(first_core, held, other), jnp.where(first_core, other, held)], axis=1
        )
    )
    forward(spec_h)

    wait_all(x_recv, 0)
    fill(x_recv[...].astype(F32))
    forward(spec_x)
    inverse(spec_x, spec_h, False)
    c_send[...] = filled().astype(BF16)
    start_all(c_send, c_recv, 4)

    wait_all(g_recv, 2)
    fill(g_recv[...].astype(F32))
    forward(spec_g)
    inverse(spec_x, spec_g, True)
    corr = filled()
    low, high = corr[:, :part], corr[:, part:]
    r_mine[...] = fold(jnp.where(first_core, high, low))
    swap = remote(r_mine, r_other, 5, {"tensor": sibling})
    swap.start()
    kept = jnp.where(first_core, low, high)
    swap.wait()
    r_send[...] = fold(kept + unfold(r_other[...])).reshape(r_send.shape)
    start_plane(r_send, r_mid, 6)

    inverse(spec_h, spec_g, True)
    b_send[...] = filled().astype(BF16)

    wait_all(r_mid, 6)
    for z in range(side):
        rows = r_mid[:, z].astype(F32)
        s_send[z] = rows[:, :part].reshape(side * side * part, span // 2).astype(BF16)
        s_send[side + z] = rows[:, part:].reshape(side * side * part, span // 2).astype(BF16)
    start_ring(s_send, s_recv, 7)
    start_all(b_send, b_recv, 8)

    wait_all(c_recv, 4)
    conv_ref[...] = gather_rows(c_recv[...]).T.astype(BF16)

    wait_all(s_recv, 7)
    some = [s_recv[z].astype(F32) + s_recv[side + z].astype(F32) for z in range(side)]
    run = side * part
    total = jnp.concatenate(
        [some[z][x * run : (x + 1) * run] for x in range(side) for z in range(side)], axis=0
    ).T
    quarter = span // 4
    t_send[...] = jnp.where(first_core, total[quarter:], total[:quarter])
    swap = remote(t_send, t_recv, 9, {"tensor": sibling})
    swap.start()
    held = jnp.where(first_core, total[:quarter], total[quarter:])
    swap.wait()
    other = t_recv[...]
    df_ref[:, : width // 2] = jnp.where(first_core, held, other)
    df_ref[:, width // 2 :] = jnp.where(first_core, other, held)

    wait_all(b_recv, 8)
    back_ref[...] = gather_rows(b_recv[...]).T.astype(BF16)


def shards(queries, keys, values, cotangent, filter_param, skip):
    span, width = queries.shape
    groups = lax.axis_size("context")
    side = round(groups ** (1 / 3))
    chans = width // groups
    part = chans // 2
    length = groups * span
    scale = 1.0 / (length * math.sqrt(length))
    tables = make_tables(groups, span)
    whole = pl.BlockSpec(memory_space=pltpu.VMEM)
    anywhere = pl.BlockSpec(memory_space=pl.ANY)
    wide = pltpu.VMEM((span, width), BF16)
    big = pltpu.VMEM((groups, chans, span), BF16)
    small = pltpu.VMEM((groups, chans, span // 2), BF16)
    ring = pltpu.VMEM((2 * side, side * side * part, span // 2), BF16)
    conv, back, filter_grad = pl.pallas_call(
        functools.partial(kernel, groups, side, scale),
        out_shape=(
            jax.ShapeDtypeStruct((span, width), BF16),
            jax.ShapeDtypeStruct((span, width), BF16),
            jax.ShapeDtypeStruct((span // 4, width), F32),
        ),
        in_specs=[anywhere] * 11,
        out_specs=(whole,) * 3,
        scratch_shapes=[wide] * 5
        + [pltpu.VMEM(t.shape, t.dtype) for t in tables]
        + [big] * 8
        + [small] * 5
        + [
            pltpu.VMEM((side, side, side, chans, span // 2), BF16),
            pltpu.VMEM((side * side, side, chans, span // 2), BF16),
            ring,
            ring,
        ]
        + [pltpu.VMEM((span // 4, width // 2), F32)] * 2
        + [pltpu.VMEM((2, groups * chans, span // 2), F32)]
        + [pltpu.VMEM((groups * chans, 2 * span), F32)] * 3
        + [pltpu.SemaphoreType.DMA((11,))]
        + [pltpu.SemaphoreType.DMA((10,))] * 2
        + [pltpu.SemaphoreType.REGULAR] * 2,
        compiler_params=pltpu.CompilerParams(
            collective_id=0, has_side_effects=True, vmem_limit_bytes=56 * 1024 * 1024
        ),
    )(queries, keys, values, cotangent, filter_param, *tables)
    wide_q, wide_k = queries.astype(F32), keys.astype(F32)
    wide_v, wide_g = values.astype(F32), cotangent.astype(F32)
    gated = (wide_k * wide_v).astype(BF16).astype(F32)
    grad_in = (wide_q * wide_g).astype(BF16).astype(F32)
    mixed = conv.astype(F32) + skip * gated
    d_gated = back.astype(F32) + skip * grad_in
    return (
        (wide_q * mixed).astype(BF16),
        (wide_g * mixed).astype(BF16),
        (d_gated * wide_v).astype(BF16),
        (d_gated * wide_k).astype(BF16),
        filter_grad,
    )


def solution(mesh):
    placed = (
        P("context", "tensor"),
        P("context", "tensor"),
        P("context", "tensor"),
        P("context", "tensor"),
        P("context", None),
        P("tensor"),
    )
    return jax.shard_map(
        shards,
        mesh=mesh,
        in_specs=placed,
        out_specs=(
            P("context", "tensor"),
            P("context", "tensor"),
            P("context", "tensor"),
            P("context", "tensor"),
            P(("context", "tensor"), None),
        ),
        check_vma=False,
    )
```

time: 93.5 us -> 81.8 us (0.87)
  Pallas kernels: 86.2 us -> 76.1 us
  local copies, waits for them, and re-layouts: 6.18 us -> 1.37 us
  other arithmetic: 0 us -> 3.5 us
    pallas_call x1, Pallas kernels: 86.2 us -> 76.1 us  [shards(): pl.pallas_call(functools.partial(kernel, groups, side, scale), out_shape=...]
    unnamed x13, local copies, waits for them, and re-layouts: 6.18 us -> 1.37 us
    convert_element_type x0 -> x1, other arithmetic: none -> 3.5 us  [shards(): (d_gated * wide_k).astype(BF16)]
where the time goes in v2:
time: 81.8 us; the launch traced here: 81.7 us
  Pallas kernels  76.1 us (93%)
  other arithmetic  3.5 us (4%)
  local copies, waits for them, and re-layouts  1.37 us (2%)
    pallas_call x1, Pallas kernels, shards(): pl.pallas_call(functools.partial(kernel, groups, side, scale), out_shape=...  76.1 us
    convert_element_type x1, other arithmetic, shards(): (d_gated * wide_k).astype(BF16)  3.5 us

profile of v2, /device:TPU:1, one launch (start us, length us, event | category | flops | bytes accessed | tf_op | source)
XLA Modules:
  0.0 81.7 jit_solution(12851739925336718345)
XLA Ops:
  0.6 0.0 copy-start.3
  0.6 0.0 copy-start.2
  0.7 0.0 copy-start
  0.7 0.0 copy-start.1
  0.7 76.1 %shard_map.155 = (bf16[256,1024]{1,0:T(8,128)(2,1)}, bf16[256,1024]{1,0:T(8,128)(2,1)}, f32[64,1024]{1,0:T(8,128)}) custom-call(bf16[256,1024]{1,0:T(8,128)(2,1)} %q_hbm.1, bf16[256,1024]{1,0:T(8,128)(2,1)} %k_hbm.1, bf16[256,1024]{1,0:T(8,128)(2,1)} %v_hbm.1, bf16[256,1024]{1,0:T(8,128)(2,1)} %g_hbm.1, bf16[256,1024]{1,0:T(8,128)(2,1)} %f_hbm.1, ...), custom_call_target="tpu_custom_call" | custom-call | tf_op jit(solution)/shard_map/pallas_call | solution.py:344
  76.8 0.0 copy-start.5
  76.8 0.0 copy-done.3
  76.8 0.0 copy-done.2
  76.8 0.0 copy-done
  76.8 0.0 copy-done.1
  76.8 0.6 copy-done.5
  77.4 0.0 copy-start.4
  77.4 3.5 %fusion.1 = (bf16[256,1024]{1,0:T(8,128)(2,1)}, bf16[256,1024]{1,0:T(8,128)(2,1)}, bf16[256,1024]{1,0:T(8,128)(2,1)}, bf16[256,1024]{1,0:T(8,128)(2,1)}) fusion(bf16[256,1024]{1,0:T(8,128)(2,1)S(1)} %copy-done, bf16[256,1024]{1,0:T(8,128)(2,1)} %get-tuple-element.9, f32[1024]{0:T(1024)S(1)} %copy-done.5, bf16[256,1024]{1,0:T(8,128)(2,1)S(1)} %copy-done.3, ...), kind=kLoop, calls=%fused_computation.7 | loop fusion | flops 6291456 | bytes 5246976 | tf_op jit(solution)/shard_map/convert_element_type | solution.py:383
  80.9 0.0 copy-done.4
  81.0 0.7 copy.18
Async XLA Ops:
  0.6 76.1 %copy-start.3 = (bf16[256,1024]{1,0:T(8,128)(2,1)S(1)}, bf16[256,1024]{1,0:T(8,128)(2,1)}, u32[]{:S(2)}) copy-start(bf16[256,1024]{1,0:T(8,128)(2,1)} %g_hbm.1) | copy-start | bytes 1572868
  0.6 76.1 %copy-start.2 = (bf16[256,1024]{1,0:T(8,128)(2,1)S(1)}, bf16[256,1024]{1,0:T(8,128)(2,1)}, u32[]{:S(2)}) copy-start(bf16[256,1024]{1,0:T(8,128)(2,1)} %v_hbm.1) | copy-start | bytes 1572868
  0.7 76.1 %copy-start = (bf16[256,1024]{1,0:T(8,128)(2,1)S(1)}, bf16[256,1024]{1,0:T(8,128)(2,1)}, u32[]{:S(2)}) copy-start(bf16[256,1024]{1,0:T(8,128)(2,1)} %k_hbm.1) | copy-start | bytes 1572868
  0.7 76.1 %copy-start.1 = (bf16[256,1024]{1,0:T(8,128)(2,1)S(1)}, bf16[256,1024]{1,0:T(8,128)(2,1)}, u32[]{:S(2)}) copy-start(bf16[256,1024]{1,0:T(8,128)(2,1)} %q_hbm.1) | copy-start | bytes 1572868
  76.8 0.7 copy-start.5
  77.4 3.5 %copy-start.4 = (f32[64,1024]{1,0:T(8,128)S(1)}, f32[64,1024]{1,0:T(8,128)}, u32[]{:S(2)}) copy-start(f32[64,1024]{1,0:T(8,128)} %get-tuple-element.24) | copy-start | bytes 786436

commit v3 on v2

--- a/solution.py
+++ b/solution.py
@@ -73,16 +73,16 @@
     groups,
     side,
     scale,
-    q_hbm, k_hbm, v_hbm, g_hbm, f_hbm,
+    q_hbm, k_hbm, v_hbm, g_hbm, f_hbm, skip_ref,
     outer_fwd_hbm, outer_inv_hbm, twist_cos_hbm, twist_sin_hbm, inner_fwd_hbm, inner_inv_hbm,
-    conv_ref, back_ref, df_ref,
+    mixed_ref, turned_ref, df_ref,
     q_ref, k_ref, v_ref, g_ref, f_ref,
     outer_fwd, outer_inv, twist_cos, twist_sin, inner_fwd, inner_inv,
     x_send, x_recv, g_send, g_recv, c_send, c_recv, b_send, b_recv,
     f_send, f_recv, f_other, r_mine, r_other,
     r_send, r_mid, s_send, s_recv, t_send, t_recv,
-    time_buf, spec_x, spec_h, spec_g,
-    load_sem, send_sem, recv_sem, ring_sem, line_sem,
+    time_buf, kept_buf, spec_x, spec_h, spec_g,
+    load_sem, send_sem, recv_sem, ring_sem,
 ):
     span, width = q_ref.shape
     chans = x_send.shape[1]
@@ -107,20 +107,11 @@
     def at_plane(p):
         return {"context": (mx * side + p % side) * side + my, "tensor": (p // side) * 2 + core}
 
-    def along_x(s):
-        return {"context": (((mx + s) % side) * side + mz) * side + my}
-
-    def along_y(s):
-        return {"context": (mx * side + mz) * side + (my + s) % side}
-
-    def along_ring(s):
-        return at_plane((plane + s) % ring)
-
-    def greet(sem, where, count):
+    def greet(sem, where, first, count):
         def body(s, carry):
             pl.semaphore_signal(sem, inc=1, device_id=where(s), device_id_type=MESH)
             return carry
-        lax.fori_loop(1, count, body, 0)
+        lax.fori_loop(first, count, body, 0)
 
     def remote(src, dst, slot, where):
         return pltpu.make_async_remote_copy(
@@ -129,12 +120,15 @@
             device_id=where, device_id_type=MESH,
         )
 
-    def start_all(src, dst, slot):
+    def start_some(src, dst, slot, first, last):
         def body(s, carry):
             to = (me + s) % groups
             remote(src.at[to], dst.at[me], slot, {"context": to}).start()
             return carry
-        lax.fori_loop(1, groups, body, 0)
+        lax.fori_loop(first, last, body, 0)
+
+    def start_all(src, dst, slot):
+        start_some(src, dst, slot, 1, groups)
         dst[pl.ds(me, 1)] = src[pl.ds(me, 1)]
 
     def start_nearest(src, dst, slot):
@@ -233,31 +227,29 @@
         load.start()
 
     barrier = pltpu.get_barrier_semaphore()
-    greet(barrier, along_x, side)
-    greet(barrier, along_y, side)
-    greet(barrier, along_ring, ring)
+    greet(barrier, lambda s: {"context": (me + s) % groups}, 1, groups)
+    greet(barrier, lambda s: at_plane((1 - upper) * side + s), 0, side)
     pl.semaphore_signal(barrier, inc=1, device_id={"tensor": sibling}, device_id_type=MESH)
     loads[0].wait()
     loads[1].wait()
     x_send[...] = spread(product(k_ref, v_ref).T, groups)
-    pl.semaphore_wait(barrier, 2 * side + ring - 2)
-    greet(ring_sem, along_ring, ring)
     loads[2].wait()
     taps = f_ref[...].astype(F32)
     taps = jnp.where(first_core, taps[:, : width // 2], taps[:, width // 2 :]).T
     f_send[...] = fold(taps.reshape(groups, part, span))
-    pl.semaphore_wait(ring_sem, ring - 1)
-    greet(line_sem, along_x, side)
-    pl.semaphore_wait(line_sem, side - 1)
-
-    start_all(x_send, x_recv, 0)
-    start_nearest(f_send, f_recv, 1)
+    pl.semaphore_wait(barrier, groups + side)
+    greet(ring_sem, lambda s: at_plane((1 - upper) * side + s), 0, side)
+    start_some(x_send, x_recv, 0, 1, groups // 2)
+    x_recv[pl.ds(me, 1)] = x_send[pl.ds(me, 1)]
     loads[3].wait()
     loads[4].wait()
     g_send[...] = spread(product(q_ref, g_ref).T, groups)
-    start_all(g_send, g_recv, 2)
     for load in loads[5:]:
         load.wait()
+    pl.semaphore_wait(ring_sem, side)
+    start_nearest(f_send, f_recv, 1)
+    start_some(x_send, x_recv, 0, groups // 2, groups)
+    start_all(g_send, g_recv, 2)
 
     wait_all(f_recv, 1)
     swap = remote(f_recv, f_other, 3, {"tensor": sibling})
@@ -276,8 +268,8 @@
     forward(spec_x)
     inverse(spec_x, spec_h, False)
     c_send[...] = filled().astype(BF16)
+
     start_all(c_send, c_recv, 4)
-
     wait_all(g_recv, 2)
     fill(g_recv[...].astype(F32))
     forward(spec_g)
@@ -287,13 +279,15 @@
     r_mine[...] = fold(jnp.where(first_core, high, low))
     swap = remote(r_mine, r_other, 5, {"tensor": sibling})
     swap.start()
-    kept = jnp.where(first_core, low, high)
-    swap.wait()
-    r_send[...] = fold(kept + unfold(r_other[...])).reshape(r_send.shape)
-    start_plane(r_send, r_mid, 6)
+    kept_buf[...] = jnp.where(first_core, low, high)
 
     inverse(spec_h, spec_g, True)
     b_send[...] = filled().astype(BF16)
+
+    swap.wait()
+    r_send[...] = fold(kept_buf[...] + unfold(r_other[...])).reshape(r_send.shape)
+    start_plane(r_send, r_mid, 6)
+    start_all(b_send, b_recv, 8)
 
     wait_all(r_mid, 6)
     for z in range(side):
@@ -301,10 +295,9 @@
         s_send[z] = rows[:, :part].reshape(side * side * part, span // 2).astype(BF16)
         s_send[side + z] = rows[:, part:].reshape(side * side * part, span // 2).astype(BF16)
     start_ring(s_send, s_recv, 7)
-    start_all(b_send, b_recv, 8)
 
     wait_all(c_recv, 4)
-    conv_ref[...] = gather_rows(c_recv[...]).T.astype(BF16)
+    mixed_ref[...] = gather_rows(c_recv[...]).T + skip_ref[...] * product(k_ref, v_ref)
 
     wait_all(s_recv, 7)
     some = [s_recv[z].astype(F32) + s_recv[side + z].astype(F32) for z in range(side)]
@@ -323,7 +316,7 @@
     df_ref[:, width // 2 :] = jnp.where(first_core, other, held)
 
     wait_all(b_recv, 8)
-    back_ref[...] = gather_rows(b_recv[...]).T.astype(BF16)
+    turned_ref[...] = gather_rows(b_recv[...]).T + skip_ref[...] * product(q_ref, g_ref)
 
 
 def shards(queries, keys, values, cotangent, filter_param, skip):
@@ -341,14 +334,14 @@
     big = pltpu.VMEM((groups, chans, span), BF16)
     small = pltpu.VMEM((groups, chans, span // 2), BF16)
     ring = pltpu.VMEM((2 * side, side * side * part, span // 2), BF16)
-    conv, back, filter_grad = pl.pallas_call(
+    mixed, turned, filter_grad = pl.pallas_call(
         functools.partial(kernel, groups, side, scale),
         out_shape=(
-            jax.ShapeDtypeStruct((span, width), BF16),
-            jax.ShapeDtypeStruct((span, width), BF16),
+            jax.ShapeDtypeStruct((span, width), F32),
+            jax.ShapeDtypeStruct((span, width), F32),
             jax.ShapeDtypeStruct((span // 4, width), F32),
         ),
-        in_specs=[anywhere] * 11,
+        in_specs=[anywhere] * 5 + [whole] + [anywhere] * 6,
         out_specs=(whole,) * 3,
         scratch_shapes=[wide] * 5
         + [pltpu.VMEM(t.shape, t.dtype) for t in tables]
@@ -362,25 +355,20 @@
         ]
         + [pltpu.VMEM((span // 4, width // 2), F32)] * 2
         + [pltpu.VMEM((2, groups * chans, span // 2), F32)]
+        + [pltpu.VMEM((groups, part, span), F32)]
         + [pltpu.VMEM((groups * chans, 2 * span), F32)] * 3
         + [pltpu.SemaphoreType.DMA((11,))]
         + [pltpu.SemaphoreType.DMA((10,))] * 2
-        + [pltpu.SemaphoreType.REGULAR] * 2,
+        + [pltpu.SemaphoreType.REGULAR],
         compiler_params=pltpu.CompilerParams(
             collective_id=0, has_side_effects=True, vmem_limit_bytes=56 * 1024 * 1024
         ),
-    )(queries, keys, values, cotangent, filter_param, *tables)
-    wide_q, wide_k = queries.astype(F32), keys.astype(F32)
-    wide_v, wide_g = values.astype(F32), cotangent.astype(F32)
-    gated = (wide_k * wide_v).astype(BF16).astype(F32)
-    grad_in = (wide_q * wide_g).astype(BF16).astype(F32)
-    mixed = conv.astype(F32) + skip * gated
-    d_gated = back.astype(F32) + skip * grad_in
+    )(queries, keys, values, cotangent, filter_param, skip.reshape(1, width), *tables)
     return (
-        (wide_q * mixed).astype(BF16),
-        (wide_g * mixed).astype(BF16),
-        (d_gated * wide_v).astype(BF16),
-        (d_gated * wide_k).astype(BF16),
+        (queries.astype(F32) * mixed).astype(BF16),
+        (cotangent.astype(F32) * mixed).astype(BF16),
+        (turned * values.astype(F32)).astype(BF16),
+        (turned * keys.astype(F32)).astype(BF16),
         filter_grad,
     )
 

time: 81.8 us -> 76.1 us (0.930)
  Pallas kernels: 76.1 us -> 71.2 us
    pallas_call x1, Pallas kernels: 76.1 us -> 71.2 us  [shards(): pl.pallas_call(functools.partial(kernel, groups, side, scale), out_shape=...]
where the time goes in v3:
time: 76.1 us; the launch traced here: 76 us
  Pallas kernels  71.2 us (94%)
  other arithmetic  3.37 us (4%)
    pallas_call x1, Pallas kernels, shards(): pl.pallas_call(functools.partial(kernel, groups, side, scale), out_shape=...  71.2 us
    convert_element_type x1, other arithmetic, shards(): (turned * keys.astype(F32)).astype(BF16)  3.37 us

profile of v3, /device:TPU:1, one launch (start us, length us, event | category | flops | bytes accessed | tf_op | source)
XLA Modules:
  0.0 76.0 jit_solution(13504483323902218203)
XLA Ops:
  0.6 0.0 copy-start
  0.6 0.0 copy-start.1
  0.7 0.0 copy-start.2
  0.7 0.0 copy-start.3
  0.7 71.2 %shard_map.155 = (f32[256,1024]{1,0:T(8,128)}, f32[256,1024]{1,0:T(8,128)}, f32[64,1024]{1,0:T(8,128)}) custom-call(bf16[256,1024]{1,0:T(8,128)(2,1)} %q_hbm.1, bf16[256,1024]{1,0:T(8,128)(2,1)} %k_hbm.1, bf16[256,1024]{1,0:T(8,128)(2,1)} %v_hbm.1, bf16[256,1024]{1,0:T(8,128)(2,1)} %g_hbm.1, bf16[256,1024]{1,0:T(8,128)(2,1)} %f_hbm.1, f32[1,1024]{1,0:T(1,128)} %bitcast.1, ...), custom_call_target="tpu_custom_call" | custom-call | tf_op jit(solution)/shard_map/pallas_call | solution.py:337
  71.8 0.0 copy-done
  71.8 0.0 copy-done.1
  71.9 0.0 copy-done.2
  71.9 0.0 copy-done.3
  71.9 0.0 copy-start.4
  71.9 3.4 %multiply_convert_fusion = (bf16[256,1024]{1,0:T(8,128)(2,1)}, bf16[256,1024]{1,0:T(8,128)(2,1)}, bf16[256,1024]{1,0:T(8,128)(2,1)}, bf16[256,1024]{1,0:T(8,128)(2,1)}) fusion(f32[256,1024]{1,0:T(8,128)} %get-tuple-element.9, bf16[256,1024]{1,0:T(8,128)(2,1)S(1)} %copy-done.1, bf16[256,1024]{1,0:T(8,128)(2,1)S(1)} %copy-done.2, ...), kind=kLoop, calls=%fused_computation | loop fusion | flops 3145728 | bytes 6291456 | tf_op jit(solution)/shard_map/convert_element_type | solution.py:371
  75.2 0.0 copy-done.4
  75.3 0.7 copy.18
Async XLA Ops:
  0.6 71.2 %copy-start = (bf16[256,1024]{1,0:T(8,128)(2,1)S(1)}, bf16[256,1024]{1,0:T(8,128)(2,1)}, u32[]{:S(2)}) copy-start(bf16[256,1024]{1,0:T(8,128)(2,1)} %q_hbm.1) | copy-start | bytes 1572868
  0.6 71.2 %copy-start.1 = (bf16[256,1024]{1,0:T(8,128)(2,1)S(1)}, bf16[256,1024]{1,0:T(8,128)(2,1)}, u32[]{:S(2)}) copy-start(bf16[256,1024]{1,0:T(8,128)(2,1)} %k_hbm.1) | copy-start | bytes 1572868
  0.7 71.2 %copy-start.2 = (bf16[256,1024]{1,0:T(8,128)(2,1)S(1)}, bf16[256,1024]{1,0:T(8,128)(2,1)}, u32[]{:S(2)}) copy-start(bf16[256,1024]{1,0:T(8,128)(2,1)} %v_hbm.1) | copy-start | bytes 1572868
  0.7 71.2 %copy-start.3 = (bf16[256,1024]{1,0:T(8,128)(2,1)S(1)}, bf16[256,1024]{1,0:T(8,128)(2,1)}, u32[]{:S(2)}) copy-start(bf16[256,1024]{1,0:T(8,128)(2,1)} %g_hbm.1) | copy-start | bytes 1572868
  71.9 3.4 %copy-start.4 = (f32[64,1024]{1,0:T(8,128)S(1)}, f32[64,1024]{1,0:T(8,128)}, u32[]{:S(2)}) copy-start(f32[64,1024]{1,0:T(8,128)} %get-tuple-element.26) | copy-start | bytes 786436

commit v4 on v3

--- a/solution.py
+++ b/solution.py
@@ -50,14 +50,6 @@
     return jnp.concatenate([first, second], axis=1).astype(BF16)
 
 
-def gather_rows(blocks):
-    groups, rows, span = blocks.shape
-    wide = blocks.astype(F32)
-    first = wide[:, : rows // 2].reshape(groups * rows // 2, span)
-    second = wide[:, rows // 2 :].reshape(groups * rows // 2, span)
-    return jnp.concatenate([first, second], axis=0)
-
-
 def fold(rows):
     half = rows.shape[2] // 2
     return jnp.concatenate([rows[:, :, :half], rows[:, :, half:]], axis=1).astype(BF16)
@@ -75,14 +67,15 @@
     scale,
     q_hbm, k_hbm, v_hbm, g_hbm, f_hbm, skip_ref,
     outer_fwd_hbm, outer_inv_hbm, twist_cos_hbm, twist_sin_hbm, inner_fwd_hbm, inner_inv_hbm,
-    mixed_ref, turned_ref, df_ref,
+    out_hbm, dq_hbm, dk_hbm, dv_hbm, df_hbm,
     q_ref, k_ref, v_ref, g_ref, f_ref,
     outer_fwd, outer_inv, twist_cos, twist_sin, inner_fwd, inner_inv,
     x_send, x_recv, g_send, g_recv, c_send, c_recv, b_send, b_recv,
     f_send, f_recv, f_other, r_mine, r_other,
     r_send, r_mid, s_send, s_recv, t_send, t_recv,
     time_buf, kept_buf, spec_x, spec_h, spec_g,
-    load_sem, send_sem, recv_sem, ring_sem,
+    out_ref, dq_ref, dk_ref, dv_ref, df_ref,
+    save_sem, load_sem, send_sem, recv_sem, ring_sem,
 ):
     span, width = q_ref.shape
     chans = x_send.shape[1]
@@ -212,6 +205,28 @@
 
     def product(a_ref, b_ref):
         return (a_ref[...].astype(F32) * b_ref[...].astype(F32)).astype(BF16).astype(F32)
+
+    def save(src, dst, n):
+        copy = pltpu.make_async_copy(src, dst, save_sem.at[n])
+        copy.start()
+        return copy
+
+    def finish(recv, left, right, results, first):
+        saves = []
+        block = width // 4
+        count = block // part
+        for n in range(4):
+            start = (n % 2) * count
+            rows = recv[start : start + count].astype(F32)
+            rows = rows[:, :part] if n < 2 else rows[:, part:]
+            cols = slice(n * block, (n + 1) * block)
+            direct = left[:, cols].astype(F32) * right[:, cols].astype(F32)
+            direct = direct.astype(BF16).astype(F32)
+            total = rows.reshape(block, span).T + skip_ref[:, cols] * direct
+            for m, (factor, held, dst) in enumerate(results):
+                held[:, cols] = (factor[:, cols].astype(F32) * total).astype(BF16)
+                saves.append(save(held.at[:, cols], dst.at[:, cols], first + 2 * n + m))
+        return saves
 
     loads = [
         pltpu.make_async_copy(src, dst, load_sem.at[n])
@@ -297,7 +312,9 @@
     start_ring(s_send, s_recv, 7)
 
     wait_all(c_recv, 4)
-    mixed_ref[...] = gather_rows(c_recv[...]).T + skip_ref[...] * product(k_ref, v_ref)
+    saves = finish(
+        c_recv, k_ref, v_ref, [(q_ref, out_ref, out_hbm), (g_ref, dq_ref, dq_hbm)], 0
+    )
 
     wait_all(s_recv, 7)
     some = [s_recv[z].astype(F32) + s_recv[side + z].astype(F32) for z in range(side)]
@@ -314,9 +331,33 @@
     other = t_recv[...]
     df_ref[:, : width // 2] = jnp.where(first_core, held, other)
     df_ref[:, width // 2 :] = jnp.where(first_core, other, held)
+    saves.append(save(df_ref, df_hbm, 16))
 
     wait_all(b_recv, 8)
-    turned_ref[...] = gather_rows(b_recv[...]).T + skip_ref[...] * product(q_ref, g_ref)
+    saves += finish(
+        b_recv, q_ref, g_ref, [(v_ref, dk_ref, dk_hbm), (k_ref, dv_ref, dv_hbm)], 8
+    )
+    for copy in saves:
+        copy.wait()
+
+
+def hand_over(*refs):
+    load_sem, save_sem = refs[15:]
+    loads, saves = [], []
+    for n in range(5):
+        src, dst, held = refs[n], refs[5 + n], refs[10 + n]
+        part = src.shape[0] // 2
+        for m in range(2):
+            rows = pl.ds(m * part, part)
+            loads.append(pltpu.make_async_copy(src.at[rows], held.at[rows], load_sem.at[n, m]))
+            saves.append(pltpu.make_async_copy(held.at[rows], dst.at[rows], save_sem.at[n, m]))
+    for load in loads:
+        load.start()
+    for load, copy in zip(loads, saves):
+        load.wait()
+        copy.start()
+    for copy in saves:
+        copy.wait()
 
 
 def shards(queries, keys, values, cotangent, filter_param, skip):
@@ -334,15 +375,13 @@
     big = pltpu.VMEM((groups, chans, span), BF16)
     small = pltpu.VMEM((groups, chans, span // 2), BF16)
     ring = pltpu.VMEM((2 * side, side * side * part, span // 2), BF16)
-    mixed, turned, filter_grad = pl.pallas_call(
+    shape = jax.ShapeDtypeStruct((span, width), BF16)
+    shapes = (shape,) * 4 + (jax.ShapeDtypeStruct((span // 4, width), F32),)
+    results = pl.pallas_call(
         functools.partial(kernel, groups, side, scale),
-        out_shape=(
-            jax.ShapeDtypeStruct((span, width), F32),
-            jax.ShapeDtypeStruct((span, width), F32),
-            jax.ShapeDtypeStruct((span // 4, width), F32),
-        ),
+        out_shape=shapes,
         in_specs=[anywhere] * 5 + [whole] + [anywhere] * 6,
-        out_specs=(whole,) * 3,
+        out_specs=(anywhere,) * 5,
         scratch_shapes=[wide] * 5
         + [pltpu.VMEM(t.shape, t.dtype) for t in tables]
         + [big] * 8
@@ -357,20 +396,23 @@
         + [pltpu.VMEM((2, groups * chans, span // 2), F32)]
         + [pltpu.VMEM((groups, part, span), F32)]
         + [pltpu.VMEM((groups * chans, 2 * span), F32)] * 3
-        + [pltpu.SemaphoreType.DMA((11,))]
+        + [wide] * 4
+        + [pltpu.VMEM((span // 4, width), F32)]
+        + [pltpu.SemaphoreType.DMA((17,)), pltpu.SemaphoreType.DMA((11,))]
         + [pltpu.SemaphoreType.DMA((10,))] * 2
         + [pltpu.SemaphoreType.REGULAR],
         compiler_params=pltpu.CompilerParams(
             collective_id=0, has_side_effects=True, vmem_limit_bytes=56 * 1024 * 1024
         ),
     )(queries, keys, values, cotangent, filter_param, skip.reshape(1, width), *tables)
-    return (
-        (queries.astype(F32) * mixed).astype(BF16),
-        (cotangent.astype(F32) * mixed).astype(BF16),
-        (turned * values.astype(F32)).astype(BF16),
-        (turned * keys.astype(F32)).astype(BF16),
-        filter_grad,
-    )
+    return pl.pallas_call(
+        hand_over,
+        out_shape=shapes,
+        in_specs=[anywhere] * 5,
+        out_specs=(anywhere,) * 5,
+        scratch_shapes=[pltpu.VMEM(r.shape, r.dtype) for r in shapes]
+        + [pltpu.SemaphoreType.DMA((5, 2))] * 2,
+    )(*results)
 
 
 def solution(mesh):

time: 76.1 us -> 74.3 us (0.976)
  other arithmetic: 3.37 us -> 0 us
  Pallas kernels: 71.2 us -> 73.5 us
    convert_element_type x1 -> x0, other arithmetic: 3.37 us -> none  [shards(): (turned * keys.astype(F32)).astype(BF16)]
    pallas_call x0 -> x1, Pallas kernels: none -> 2.51 us  [shards(): pl.pallas_call(hand_over, out_shape=shapes, in_specs=[anywhere] * 5, out_...]
where the time goes in v4:
time: 74.3 us; the launch traced here: 74.2 us
  Pallas kernels  73.5 us (99%)
    pallas_call x1, Pallas kernels, shards(): pl.pallas_call(functools.partial(kernel, groups, side, scale), out_shape=...  71 us
    pallas_call x1, Pallas kernels, shards(): pl.pallas_call(hand_over, out_shape=shapes, in_specs=[anywhere] * 5, out_...  2.51 us

profile of v4, /device:TPU:1, one launch (start us, length us, event | category | flops | bytes accessed | tf_op | source)
XLA Modules:
  0.0 74.2 jit_solution(5306486026646588157)
XLA Ops:
  0.6 71.0 %shard_map.155 = (bf16[256,1024]{1,0:T(8,128)(2,1)}, bf16[256,1024]{1,0:T(8,128)(2,1)}, bf16[256,1024]{1,0:T(8,128)(2,1)}, bf16[256,1024]{1,0:T(8,128)(2,1)}, f32[64,1024]{1,0:T(8,128)}) custom-call(bf16[256,1024]{1,0:T(8,128)(2,1)} %q_hbm.1, bf16[256,1024]{1,0:T(8,128)(2,1)} %k_hbm.1, bf16[256,1024]{1,0:T(8,128)(2,1)} %v_hbm.1, bf16[256,1024]{1,0:T(8,128)(2,1)} %g_hbm.1, ...), custom_call_target="tpu_custom_call" | custom-call | tf_op jit(solution)/shard_map/pallas_call | solution.py:380
  71.7 2.5 %shard_map.156 = (bf16[256,1024]{1,0:T(8,128)(2,1)}, bf16[256,1024]{1,0:T(8,128)(2,1)}, bf16[256,1024]{1,0:T(8,128)(2,1)}, bf16[256,1024]{1,0:T(8,128)(2,1)}, f32[64,1024]{1,0:T(8,128)}) custom-call(bf16[256,1024]{1,0:T(8,128)(2,1)} %get-tuple-element.10.refs_0_, bf16[256,1024]{1,0:T(8,128)(2,1)} %get-tuple-element.11.refs_1_, ...), custom_call_target="tpu_custom_call" | custom-call | tf_op jit(solution)/shard_map/pallas_call | solution.py:408

commit v5 on v4

--- a/solution.py
+++ b/solution.py
@@ -70,9 +70,10 @@
     out_hbm, dq_hbm, dk_hbm, dv_hbm, df_hbm,
     q_ref, k_ref, v_ref, g_ref, f_ref,
     outer_fwd, outer_inv, twist_cos, twist_sin, inner_fwd, inner_inv,
-    x_send, x_recv, g_send, g_recv, c_send, c_recv, b_send, b_recv,
+    x_send, x_recv, g_send, g_recv,
+    c0_send, c0_recv, c1_send, c1_recv, b0_send, b0_recv, b1_send, b1_recv,
     f_send, f_recv, f_other, r_mine, r_other,
-    r_send, r_mid, s_send, s_recv, t_send, t_recv,
+    r_send, r_mid, s_send, s_recv, t_send, t_recv, own_buf,
     time_buf, kept_buf, spec_x, spec_h, spec_g,
     out_ref, dq_ref, dk_ref, dv_ref, df_ref,
     save_sem, load_sem, send_sem, recv_sem, ring_sem,
@@ -158,11 +159,12 @@
         time_buf[0] = flat[:, : span // 2]
         time_buf[1] = flat[:, span // 2 :]
 
-    def filled():
-        flat = jnp.concatenate([time_buf[0], time_buf[1]], axis=1)
-        return flat.reshape(groups, chans, span)
-
-    def forward(dst):
+    def packed(n):
+        low = time_buf[0].reshape(groups, chans, span // 2)[:, n * part : (n + 1) * part]
+        high = time_buf[1].reshape(groups, chans, span // 2)[:, n * part : (n + 1) * part]
+        return jnp.concatenate([low, high], axis=1)
+
+    def forward(dst, first=0, last=chans // step):
         def body(n, carry):
             parts = []
             for c in range(step):
@@ -178,9 +180,9 @@
             here = pl.ds(pl.multiple_of(n * step * groups, step * groups), step * groups)
             dst[here, :] = dot(rows, inner_fwd[...])
             return carry
-        lax.fori_loop(0, chans // step, body, 0)
-
-    def inverse(a_ref, b_ref, conj):
+        lax.fori_loop(first, last, body, 0)
+
+    def inverse(a_ref, b_ref, conj, first=0, last=chans // step):
         def body(n, carry):
             here = pl.ds(pl.multiple_of(n * step * groups, step * groups), step * groups)
             ar, ai = a_ref[here, :span], a_ref[here, span:]
@@ -201,7 +203,7 @@
                 time_buf[0, rows, :] = field[:, : span // 2]
                 time_buf[1, rows, :] = field[:, span // 2 :]
             return carry
-        lax.fori_loop(0, chans // step, body, 0)
+        lax.fori_loop(first, last, body, 0)
 
     def product(a_ref, b_ref):
         return (a_ref[...].astype(F32) * b_ref[...].astype(F32)).astype(BF16).astype(F32)
@@ -211,14 +213,13 @@
         copy.start()
         return copy
 
-    def finish(recv, left, right, results, first):
+    def finish(half, recv, left, right, results, first):
         saves = []
         block = width // 4
         count = block // part
-        for n in range(4):
+        for n in (2 * half, 2 * half + 1):
             start = (n % 2) * count
-            rows = recv[start : start + count].astype(F32)
-            rows = rows[:, :part] if n < 2 else rows[:, part:]
+            rows = unfold(recv[start : start + count])
             cols = slice(n * block, (n + 1) * block)
             direct = left[:, cols].astype(F32) * right[:, cols].astype(F32)
             direct = direct.astype(BF16).astype(F32)
@@ -280,29 +281,35 @@
 
     wait_all(x_recv, 0)
     fill(x_recv[...].astype(F32))
-    forward(spec_x)
-    inverse(spec_x, spec_h, False)
-    c_send[...] = filled().astype(BF16)
-
-    start_all(c_send, c_recv, 4)
+    mid = chans // step // 2
+    forward(spec_x, 0, mid)
+    inverse(spec_x, spec_h, False, 0, mid)
+    c0_send[...] = packed(0).astype(BF16)
+    start_all(c0_send, c0_recv, 4)
+    forward(spec_x, mid, 2 * mid)
+    inverse(spec_x, spec_h, False, mid, 2 * mid)
+    c1_send[...] = packed(1).astype(BF16)
+    start_all(c1_send, c1_recv, 10)
+
     wait_all(g_recv, 2)
     fill(g_recv[...].astype(F32))
     forward(spec_g)
     inverse(spec_x, spec_g, True)
-    corr = filled()
-    low, high = corr[:, :part], corr[:, part:]
-    r_mine[...] = fold(jnp.where(first_core, high, low))
+    low, high = packed(0), packed(1)
+    r_mine[...] = jnp.where(first_core, high, low).astype(BF16)
     swap = remote(r_mine, r_other, 5, {"tensor": sibling})
     swap.start()
     kept_buf[...] = jnp.where(first_core, low, high)
 
-    inverse(spec_h, spec_g, True)
-    b_send[...] = filled().astype(BF16)
-
+    inverse(spec_h, spec_g, True, 0, mid)
+    b0_send[...] = packed(0).astype(BF16)
     swap.wait()
-    r_send[...] = fold(kept_buf[...] + unfold(r_other[...])).reshape(r_send.shape)
+    r_send[...] = (kept_buf[...] + r_other[...].astype(F32)).astype(BF16).reshape(r_send.shape)
     start_plane(r_send, r_mid, 6)
-    start_all(b_send, b_recv, 8)
+    start_all(b0_send, b0_recv, 8)
+    inverse(spec_h, spec_g, True, mid, 2 * mid)
+    b1_send[...] = packed(1).astype(BF16)
+    start_all(b1_send, b1_recv, 11)
 
     wait_all(r_mid, 6)
     for z in range(side):
@@ -311,10 +318,14 @@
         s_send[side + z] = rows[:, part:].reshape(side * side * part, span // 2).astype(BF16)
     start_ring(s_send, s_recv, 7)
 
-    wait_all(c_recv, 4)
-    saves = finish(
-        c_recv, k_ref, v_ref, [(q_ref, out_ref, out_hbm), (g_ref, dq_ref, dq_hbm)], 0
-    )
+    forth = [(q_ref, out_ref, out_hbm), (g_ref, dq_ref, dq_hbm)]
+    back = [(v_ref, dk_ref, dk_hbm), (k_ref, dv_ref, dv_hbm)]
+    wait_all(c0_recv, 4)
+    saves = finish(0, c0_recv, k_ref, v_ref, forth, 0)
+    wait_all(c1_recv, 10)
+    saves += finish(1, c1_recv, k_ref, v_ref, forth, 0)
+    wait_all(b0_recv, 8)
+    saves += finish(0, b0_recv, q_ref, g_ref, back, 8)
 
     wait_all(s_recv, 7)
     some = [s_recv[z].astype(F32) + s_recv[side + z].astype(F32) for z in range(side)]
@@ -326,17 +337,14 @@
     t_send[...] = jnp.where(first_core, total[quarter:], total[:quarter])
     swap = remote(t_send, t_recv, 9, {"tensor": sibling})
     swap.start()
-    held = jnp.where(first_core, total[:quarter], total[quarter:])
+    own_buf[...] = jnp.where(first_core, total[:quarter], total[quarter:])
+    wait_all(b1_recv, 11)
+    saves += finish(1, b1_recv, q_ref, g_ref, back, 8)
     swap.wait()
-    other = t_recv[...]
+    held, other = own_buf[...], t_recv[...]
     df_ref[:, : width // 2] = jnp.where(first_core, held, other)
     df_ref[:, width // 2 :] = jnp.where(first_core, other, held)
     saves.append(save(df_ref, df_hbm, 16))
-
-    wait_all(b_recv, 8)
-    saves += finish(
-        b_recv, q_ref, g_ref, [(v_ref, dk_ref, dk_hbm), (k_ref, dv_ref, dv_hbm)], 8
-    )
     for copy in saves:
         copy.wait()
 
@@ -384,22 +392,22 @@
         out_specs=(anywhere,) * 5,
         scratch_shapes=[wide] * 5
         + [pltpu.VMEM(t.shape, t.dtype) for t in tables]
-        + [big] * 8
-        + [small] * 5
+        + [big] * 4
+        + [small] * 13
         + [
             pltpu.VMEM((side, side, side, chans, span // 2), BF16),
             pltpu.VMEM((side * side, side, chans, span // 2), BF16),
             ring,
             ring,
         ]
-        + [pltpu.VMEM((span // 4, width // 2), F32)] * 2
+        + [pltpu.VMEM((span // 4, width // 2), F32)] * 3
         + [pltpu.VMEM((2, groups * chans, span // 2), F32)]
-        + [pltpu.VMEM((groups, part, span), F32)]
+        + [pltpu.VMEM((groups, chans, span // 2), F32)]
         + [pltpu.VMEM((groups * chans, 2 * span), F32)] * 3
         + [wide] * 4
         + [pltpu.VMEM((span // 4, width), F32)]
         + [pltpu.SemaphoreType.DMA((17,)), pltpu.SemaphoreType.DMA((11,))]
-        + [pltpu.SemaphoreType.DMA((10,))] * 2
+        + [pltpu.SemaphoreType.DMA((12,))] * 2
         + [pltpu.SemaphoreType.REGULAR],
         compiler_params=pltpu.CompilerParams(
             collective_id=0, has_side_effects=True, vmem_limit_bytes=56 * 1024 * 1024

time: 74.3 us -> 72.4 us (0.974)
  Pallas kernels: 73.5 us -> 71.6 us
    pallas_call x1, Pallas kernels: 71 us -> 69.1 us  [shards(): pl.pallas_call(functools.partial(kernel, groups, side, scale), out_shape=...]
where the time goes in v5:
time: 72.4 us; the launch traced here: 72.3 us
  Pallas kernels  71.6 us (99%)
    pallas_call x1, Pallas kernels, shards(): pl.pallas_call(functools.partial(kernel, groups, side, scale), out_shape=...  69.1 us
    pallas_call x1, Pallas kernels, shards(): pl.pallas_call(hand_over, out_shape=shapes, in_specs=[anywhere] * 5, out_...  2.51 us

profile of v5, /device:TPU:1, one launch (start us, length us, event | category | flops | bytes accessed | tf_op | source)
XLA Modules:
  0.0 72.3 jit_solution(11639331969370622462)
XLA Ops:
  0.6 69.1 %shard_map.155 = (bf16[256,1024]{1,0:T(8,128)(2,1)}, bf16[256,1024]{1,0:T(8,128)(2,1)}, bf16[256,1024]{1,0:T(8,128)(2,1)}, bf16[256,1024]{1,0:T(8,128)(2,1)}, f32[64,1024]{1,0:T(8,128)}) custom-call(bf16[256,1024]{1,0:T(8,128)(2,1)} %q_hbm.1, bf16[256,1024]{1,0:T(8,128)(2,1)} %k_hbm.1, bf16[256,1024]{1,0:T(8,128)(2,1)} %v_hbm.1, bf16[256,1024]{1,0:T(8,128)(2,1)} %g_hbm.1, ...), custom_call_target="tpu_custom_call" | custom-call | tf_op jit(solution)/shard_map/pallas_call | solution.py:388
  69.8 2.5 %shard_map.156 = (bf16[256,1024]{1,0:T(8,128)(2,1)}, bf16[256,1024]{1,0:T(8,128)(2,1)}, bf16[256,1024]{1,0:T(8,128)(2,1)}, bf16[256,1024]{1,0:T(8,128)(2,1)}, f32[64,1024]{1,0:T(8,128)}) custom-call(bf16[256,1024]{1,0:T(8,128)(2,1)} %get-tuple-element.10.refs_0_, bf16[256,1024]{1,0:T(8,128)(2,1)} %get-tuple-element.11.refs_1_, ...), custom_call_target="tpu_custom_call" | custom-call | tf_op jit(solution)/shard_map/pallas_call | solution.py:416

commit v6 on v5

--- a/solution.py
+++ b/solution.py
@@ -73,7 +73,7 @@
     x_send, x_recv, g_send, g_recv,
     c0_send, c0_recv, c1_send, c1_recv, b0_send, b0_recv, b1_send, b1_recv,
     f_send, f_recv, f_other, r_mine, r_other,
-    r_send, r_mid, s_send, s_recv, t_send, t_recv, own_buf,
+    e_send, e_recv, e_kept, r_send, r_mid, s_send, s_recv, t_send, t_recv, own_buf,
     time_buf, kept_buf, spec_x, spec_h, spec_g,
     out_ref, dq_ref, dk_ref, dv_ref, df_ref,
     save_sem, load_sem, send_sem, recv_sem, ring_sem,
@@ -81,7 +81,6 @@
     span, width = q_ref.shape
     chans = x_send.shape[1]
     part = chans // 2
-    ring = 2 * side
     step = min(4, chans)
     me = lax.axis_index("context")
     mine = lax.axis_index("tensor")
@@ -89,10 +88,19 @@
     upper = mine // 2
     sibling = mine + 1 - 2 * core
     mx, mz, my = me // (side * side), (me // side) % side, me % side
-    plane = upper * side + mz
     place = mx * side + my
     near = (mz // (side // 2) + upper) % 2
     first_core = core == 0
+    first_half = upper == 0
+
+    def level_of(z, up):
+        return (z + up * (side // 2)) % side
+
+    def group_of(to, up):
+        x, z, y = to // (side * side), (to // side) % side, to % side
+        return (x * side + level_of(z, up)) * side + y
+
+    own = group_of(me, upper)
 
     def at_place(s):
         x, y = s // side, s % side
@@ -117,38 +125,47 @@
     def start_some(src, dst, slot, first, last):
         def body(s, carry):
             to = (me + s) % groups
-            remote(src.at[to], dst.at[me], slot, {"context": to}).start()
+            remote(src.at[group_of(to, upper)], dst.at[me], slot, {"context": to}).start()
             return carry
         lax.fori_loop(first, last, body, 0)
 
-    def start_all(src, dst, slot):
+    def start_out(src, dst, slot):
         start_some(src, dst, slot, 1, groups)
-        dst[pl.ds(me, 1)] = src[pl.ds(me, 1)]
+        dst[pl.ds(me, 1)] = src[pl.ds(own, 1)]
+
+    def start_home(src, dst, slot):
+        def body(s, carry):
+            to = (me + s) % groups
+            remote(src.at[to], dst.at[own], slot, {"context": to}).start()
+            return carry
+        lax.fori_loop(1, groups, body, 0)
+        dst[pl.ds(own, 1)] = src[pl.ds(me, 1)]
 
     def start_nearest(src, dst, slot):
         def body(s, carry):
             to = (me + s) % groups
             up = (near + ((to // side) % side) // (side // 2)) % 2
-            remote(src.at[to], dst.at[me], slot, {"context": to, "tensor": 2 * up + core}).start()
+            where = {"context": to, "tensor": 2 * up + core}
+            remote(src.at[group_of(to, up)], dst.at[me], slot, where).start()
             return carry
         lax.fori_loop(1, groups, body, 0)
-        dst[pl.ds(me, 1)] = src[pl.ds(me, 1)]
+        dst[pl.ds(me, 1)] = src[pl.ds(own, 1)]
 
     def start_plane(src, dst, slot):
         def body(s, carry):
             to = (place + s) % (side * side)
-            remote(src.at[to // side, :, to % side], dst.at[place], slot, at_place(to)).start()
+            remote(src.at[to], dst.at[place], slot, at_place(to)).start()
             return carry
         lax.fori_loop(1, side * side, body, 0)
-        dst[pl.ds(place, 1)] = src[pl.ds(mx, 1), :, my]
-
-    def start_ring(src, dst, slot):
-        def body(s, carry):
-            to = (plane + s) % ring
-            remote(src.at[to], dst.at[plane], slot, at_plane(to)).start()
-            return carry
-        lax.fori_loop(1, ring, body, 0)
-        dst[pl.ds(plane, 1)] = src[pl.ds(plane, 1)]
+        dst[pl.ds(place, 1)] = src[pl.ds(place, 1)]
+
+    def start_line(src, dst, slot):
+        def body(s, carry):
+            to = (mz + s) % side
+            remote(src.at[to], dst.at[level_of(mz, upper)], slot, at_plane(upper * side + to)).start()
+            return carry
+        lax.fori_loop(1, side, body, 0)
+        dst[pl.ds(level_of(mz, upper), 1)] = src[pl.ds(mz, 1)]
 
     def wait_all(dst, slot):
         blocks = dst.at[pl.ds(0, dst.shape[0] - 1)]
@@ -256,7 +273,7 @@
     pl.semaphore_wait(barrier, groups + side)
     greet(ring_sem, lambda s: at_plane((1 - upper) * side + s), 0, side)
     start_some(x_send, x_recv, 0, 1, groups // 2)
-    x_recv[pl.ds(me, 1)] = x_send[pl.ds(me, 1)]
+    x_recv[pl.ds(me, 1)] = x_send[pl.ds(own, 1)]
     loads[3].wait()
     loads[4].wait()
     g_send[...] = spread(product(q_ref, g_ref).T, groups)
@@ -265,7 +282,7 @@
     pl.semaphore_wait(ring_sem, side)
     start_nearest(f_send, f_recv, 1)
     start_some(x_send, x_recv, 0, groups // 2, groups)
-    start_all(g_send, g_recv, 2)
+    start_out(g_send, g_recv, 2)
 
     wait_all(f_recv, 1)
     swap = remote(f_recv, f_other, 3, {"tensor": sibling})
@@ -285,11 +302,11 @@
     forward(spec_x, 0, mid)
     inverse(spec_x, spec_h, False, 0, mid)
     c0_send[...] = packed(0).astype(BF16)
-    start_all(c0_send, c0_recv, 4)
+    start_home(c0_send, c0_recv, 4)
     forward(spec_x, mid, 2 * mid)
     inverse(spec_x, spec_h, False, mid, 2 * mid)
     c1_send[...] = packed(1).astype(BF16)
-    start_all(c1_send, c1_recv, 10)
+    start_home(c1_send, c1_recv, 10)
 
     wait_all(g_recv, 2)
     fill(g_recv[...].astype(F32))
@@ -304,31 +321,44 @@
     inverse(spec_h, spec_g, True, 0, mid)
     b0_send[...] = packed(0).astype(BF16)
     swap.wait()
-    r_send[...] = (kept_buf[...] + r_other[...].astype(F32)).astype(BF16).reshape(r_send.shape)
-    start_plane(r_send, r_mid, 6)
-    start_all(b0_send, b0_recv, 8)
+    total = kept_buf[...] + r_other[...].astype(F32)
+    low, high = total[:, :part], total[:, part:]
+    e_send[...] = jnp.where(first_half, high, low).reshape(e_send.shape).astype(BF16)
+    partner = at_plane((1 - upper) * side + (mz + side // 2) % side)
+    trade = remote(e_send, e_recv, 12, partner)
+    trade.start()
+    e_kept[...] = jnp.where(first_half, low, high).reshape(e_kept.shape)
+    start_home(b0_send, b0_recv, 8)
     inverse(spec_h, spec_g, True, mid, 2 * mid)
     b1_send[...] = packed(1).astype(BF16)
-    start_all(b1_send, b1_recv, 11)
-
-    wait_all(r_mid, 6)
-    for z in range(side):
-        rows = r_mid[:, z].astype(F32)
-        s_send[z] = rows[:, :part].reshape(side * side * part, span // 2).astype(BF16)
-        s_send[side + z] = rows[:, part:].reshape(side * side * part, span // 2).astype(BF16)
-    start_ring(s_send, s_recv, 7)
+    start_home(b1_send, b1_recv, 11)
+
+    trade.wait()
+    total = (e_kept[...] + e_recv[...].astype(F32)).reshape(side, side, side, part, span // 2)
+    for x in range(side):
+        for y in range(side):
+            r_send[x * side + y] = jnp.concatenate(
+                [total[x, z, y] for z in range(side)], axis=0
+            ).astype(BF16)
+    start_plane(r_send, r_mid, 6)
 
     forth = [(q_ref, out_ref, out_hbm), (g_ref, dq_ref, dq_hbm)]
     back = [(v_ref, dk_ref, dk_hbm), (k_ref, dv_ref, dv_hbm)]
     wait_all(c0_recv, 4)
     saves = finish(0, c0_recv, k_ref, v_ref, forth, 0)
+    wait_all(r_mid, 6)
+    rows = r_mid[...].astype(F32)
+    for z in range(side):
+        level = rows[:, z * part : (z + 1) * part]
+        s_send[z] = level.reshape(side * side * part, span // 2).astype(BF16)
+    start_line(s_send, s_recv, 7)
     wait_all(c1_recv, 10)
     saves += finish(1, c1_recv, k_ref, v_ref, forth, 0)
     wait_all(b0_recv, 8)
     saves += finish(0, b0_recv, q_ref, g_ref, back, 8)
 
     wait_all(s_recv, 7)
-    some = [s_recv[z].astype(F32) + s_recv[side + z].astype(F32) for z in range(side)]
+    some = [s_recv[z].astype(F32) for z in range(side)]
     run = side * part
     total = jnp.concatenate(
         [some[z][x * run : (x + 1) * run] for x in range(side) for z in range(side)], axis=0
@@ -382,7 +412,8 @@
     wide = pltpu.VMEM((span, width), BF16)
     big = pltpu.VMEM((groups, chans, span), BF16)
     small = pltpu.VMEM((groups, chans, span // 2), BF16)
-    ring = pltpu.VMEM((2 * side, side * side * part, span // 2), BF16)
+    rows = pltpu.VMEM((groups * part, span // 2), BF16)
+    line = pltpu.VMEM((side, side * side * part, span // 2), BF16)
     shape = jax.ShapeDtypeStruct((span, width), BF16)
     shapes = (shape,) * 4 + (jax.ShapeDtypeStruct((span // 4, width), F32),)
     results = pl.pallas_call(
@@ -395,10 +426,13 @@
         + [big] * 4
         + [small] * 13
         + [
-            pltpu.VMEM((side, side, side, chans, span // 2), BF16),
-            pltpu.VMEM((side * side, side, chans, span // 2), BF16),
-            ring,
-            ring,
+            rows,
+            rows,
+            pltpu.VMEM((groups * part, span // 2), F32),
+            pltpu.VMEM((side * side, side * part, span // 2), BF16),
+            pltpu.VMEM((side * side, side * part, span // 2), BF16),
+            line,
+            line,
         ]
         + [pltpu.VMEM((span // 4, width // 2), F32)] * 3
         + [pltpu.VMEM((2, groups * chans, span // 2), F32)]
@@ -407,7 +441,7 @@
         + [wide] * 4
         + [pltpu.VMEM((span // 4, width), F32)]
         + [pltpu.SemaphoreType.DMA((17,)), pltpu.SemaphoreType.DMA((11,))]
-        + [pltpu.SemaphoreType.DMA((12,))] * 2
+        + [pltpu.SemaphoreType.DMA((13,))] * 2
         + [pltpu.SemaphoreType.REGULAR],
         compiler_params=pltpu.CompilerParams(
             collective_id=0, has_side_effects=True, vmem_limit_bytes=56 * 1024 * 1024

time: 72.4 us -> 70.7 us (0.977)
  Pallas kernels: 71.6 us -> 69.9 us
    pallas_call x1, Pallas kernels: 69.1 us -> 67.4 us  [shards(): pl.pallas_call(functools.partial(kernel, groups, side, scale), out_shape=...]
where the time goes in v6:
time: 70.7 us; the launch traced here: 70.6 us
  Pallas kernels  69.9 us (99%)
    pallas_call x1, Pallas kernels, shards(): pl.pallas_call(functools.partial(kernel, groups, side, scale), out_shape=...  67.4 us
    pallas_call x1, Pallas kernels, shards(): pl.pallas_call(hand_over, out_shape=shapes, in_specs=[anywhere] * 5, out_...  2.51 us

profile of v6, /device:TPU:1, one launch (start us, length us, event | category | flops | bytes accessed | tf_op | source)
XLA Modules:
  0.0 70.6 jit_solution(7022467874395002388)
XLA Ops:
  0.6 67.4 %shard_map.155 = (bf16[256,1024]{1,0:T(8,128)(2,1)}, bf16[256,1024]{1,0:T(8,128)(2,1)}, bf16[256,1024]{1,0:T(8,128)(2,1)}, bf16[256,1024]{1,0:T(8,128)(2,1)}, f32[64,1024]{1,0:T(8,128)}) custom-call(bf16[256,1024]{1,0:T(8,128)(2,1)} %q_hbm.1, bf16[256,1024]{1,0:T(8,128)(2,1)} %k_hbm.1, bf16[256,1024]{1,0:T(8,128)(2,1)} %v_hbm.1, bf16[256,1024]{1,0:T(8,128)(2,1)} %g_hbm.1, ...), custom_call_target="tpu_custom_call" | custom-call | tf_op jit(solution)/shard_map/pallas_call | solution.py:419
  68.0 2.5 %shard_map.156 = (bf16[256,1024]{1,0:T(8,128)(2,1)}, bf16[256,1024]{1,0:T(8,128)(2,1)}, bf16[256,1024]{1,0:T(8,128)(2,1)}, bf16[256,1024]{1,0:T(8,128)(2,1)}, f32[64,1024]{1,0:T(8,128)}) custom-call(bf16[256,1024]{1,0:T(8,128)(2,1)} %get-tuple-element.10.refs_0_, bf16[256,1024]{1,0:T(8,128)(2,1)} %get-tuple-element.11.refs_1_, ...), custom_call_target="tpu_custom_call" | custom-call | tf_op jit(solution)/shard_map/pallas_call | solution.py:450

commit v7 on v6

--- a/solution.py
+++ b/solution.py
@@ -73,14 +73,17 @@
     x_send, x_recv, g_send, g_recv,
     c0_send, c0_recv, c1_send, c1_recv, b0_send, b0_recv, b1_send, b1_recv,
     f_send, f_recv, f_other, r_mine, r_other,
-    e_send, e_recv, e_kept, r_send, r_mid, s_send, s_recv, t_send, t_recv, own_buf,
+    e0_send, e1_send, e0_recv, e1_recv, e_kept, r0_send, r1_send, r0_mid, r1_mid, s_send, s_recv, t_send, t_recv, own_buf,
     time_buf, kept_buf, spec_x, spec_h, spec_g,
     out_ref, dq_ref, dk_ref, dv_ref, df_ref,
     save_sem, load_sem, send_sem, recv_sem, ring_sem,
 ):
+    e_send, e_recv = (e0_send, e1_send), (e0_recv, e1_recv)
+    r_send, r_mid = (r0_send, r1_send), (r0_mid, r1_mid)
     span, width = q_ref.shape
     chans = x_send.shape[1]
     part = chans // 2
+    half = side // 2
     step = min(4, chans)
     me = lax.axis_index("context")
     mine = lax.axis_index("tensor")
@@ -159,13 +162,17 @@
         lax.fori_loop(1, side * side, body, 0)
         dst[pl.ds(place, 1)] = src[pl.ds(place, 1)]
 
-    def start_line(src, dst, slot):
+    def start_line(src, dst, slot, first):
         def body(s, carry):
-            to = (mz + s) % side
-            remote(src.at[to], dst.at[level_of(mz, upper)], slot, at_plane(upper * side + to)).start()
-            return carry
-        lax.fori_loop(1, side, body, 0)
-        dst[pl.ds(level_of(mz, upper), 1)] = src[pl.ds(mz, 1)]
+            to = first + s
+
+            @pl.when(to != mz)
+            def _():
+                where = at_plane(upper * side + to)
+                remote(src.at[to], dst.at[level_of(mz, upper)], slot, where).start()
+
+            return carry
+        lax.fori_loop(0, side // 2, body, 0)
 
     def wait_all(dst, slot):
         blocks = dst.at[pl.ds(0, dst.shape[0] - 1)]
@@ -323,35 +330,42 @@
     swap.wait()
     total = kept_buf[...] + r_other[...].astype(F32)
     low, high = total[:, :part], total[:, part:]
-    e_send[...] = jnp.where(first_half, high, low).reshape(e_send.shape).astype(BF16)
+    cut = (side, side, side, part, span // 2)
+    sent = jnp.where(first_half, high, low).reshape(cut)
+    kept = jnp.where(first_half, low, high).reshape(cut)
     partner = at_plane((1 - upper) * side + (mz + side // 2) % side)
-    trade = remote(e_send, e_recv, 12, partner)
-    trade.start()
-    e_kept[...] = jnp.where(first_half, low, high).reshape(e_kept.shape)
+    trades = []
+    for h in range(2):
+        for z in range(half):
+            e_send[h][z] = sent[:, h * half + z].reshape(e_send[h].shape[1:]).astype(BF16)
+            e_kept[h, z] = kept[:, h * half + z].reshape(e_send[h].shape[1:])
+        trades.append(remote(e_send[h], e_recv[h], 12 + h, partner))
+        trades[h].start()
     start_home(b0_send, b0_recv, 8)
     inverse(spec_h, spec_g, True, mid, 2 * mid)
     b1_send[...] = packed(1).astype(BF16)
     start_home(b1_send, b1_recv, 11)
 
-    trade.wait()
-    total = (e_kept[...] + e_recv[...].astype(F32)).reshape(side, side, side, part, span // 2)
-    for x in range(side):
-        for y in range(side):
-            r_send[x * side + y] = jnp.concatenate(
-                [total[x, z, y] for z in range(side)], axis=0
-            ).astype(BF16)
-    start_plane(r_send, r_mid, 6)
+    for h in range(2):
+        trades[h].wait()
+        total = e_kept[h] + e_recv[h][...].astype(F32)
+        total = total.reshape(half, side * side, part, span // 2)
+        for to in range(side * side):
+            r_send[h][to] = jnp.concatenate([total[z, to] for z in range(half)], axis=0).astype(BF16)
+        start_plane(r_send[h], r_mid[h], 6 + 8 * h)
 
     forth = [(q_ref, out_ref, out_hbm), (g_ref, dq_ref, dq_hbm)]
     back = [(v_ref, dk_ref, dk_hbm), (k_ref, dv_ref, dv_hbm)]
     wait_all(c0_recv, 4)
     saves = finish(0, c0_recv, k_ref, v_ref, forth, 0)
-    wait_all(r_mid, 6)
-    rows = r_mid[...].astype(F32)
-    for z in range(side):
-        level = rows[:, z * part : (z + 1) * part]
-        s_send[z] = level.reshape(side * side * part, span // 2).astype(BF16)
-    start_line(s_send, s_recv, 7)
+    for h in range(2):
+        wait_all(r_mid[h], 6 + 8 * h)
+        rows = r_mid[h][...].astype(F32)
+        for z in range(half):
+            level = rows[:, z * part : (z + 1) * part]
+            s_send[h * half + z] = level.reshape(side * side * part, span // 2).astype(BF16)
+        start_line(s_send, s_recv, 7, h * half)
+    s_recv[pl.ds(level_of(mz, upper), 1)] = s_send[pl.ds(mz, 1)]
     wait_all(c1_recv, 10)
     saves += finish(1, c1_recv, k_ref, v_ref, forth, 0)
     wait_all(b0_recv, 8)
@@ -412,7 +426,8 @@
     wide = pltpu.VMEM((span, width), BF16)
     big = pltpu.VMEM((groups, chans, span), BF16)
     small = pltpu.VMEM((groups, chans, span // 2), BF16)
-    rows = pltpu.VMEM((groups * part, span // 2), BF16)
+    rows = pltpu.VMEM((side // 2, side * side * part, span // 2), BF16)
+    chunk = pltpu.VMEM((side * side, side // 2 * part, span // 2), BF16)
     line = pltpu.VMEM((side, side * side * part, span // 2), BF16)
     shape = jax.ShapeDtypeStruct((span, width), BF16)
     shapes = (shape,) * 4 + (jax.ShapeDtypeStruct((span // 4, width), F32),)
@@ -428,9 +443,13 @@
         + [
             rows,
             rows,
-            pltpu.VMEM((groups * part, span // 2), F32),
-            pltpu.VMEM((side * side, side * part, span // 2), BF16),
-            pltpu.VMEM((side * side, side * part, span // 2), BF16),
+            rows,
+            rows,
+            pltpu.VMEM((2, side // 2, side * side * part, span // 2), F32),
+            chunk,
+            chunk,
+            chunk,
+            chunk,
             line,
             line,
         ]
@@ -441,7 +460,7 @@
         + [wide] * 4
         + [pltpu.VMEM((span // 4, width), F32)]
         + [pltpu.SemaphoreType.DMA((17,)), pltpu.SemaphoreType.DMA((11,))]
-        + [pltpu.SemaphoreType.DMA((13,))] * 2
+        + [pltpu.SemaphoreType.DMA((15,))] * 2
         + [pltpu.SemaphoreType.REGULAR],
         compiler_params=pltpu.CompilerParams(
             collective_id=0, has_side_effects=True, vmem_limit_bytes=56 * 1024 * 1024

time: 70.7 us -> 68 us (0.962)
  Pallas kernels: 69.9 us -> 67.2 us
    pallas_call x1, Pallas kernels: 67.4 us -> 64.7 us  [shards(): pl.pallas_call(functools.partial(kernel, groups, side, scale), out_shape=...]
where the time goes in v7:
time: 68 us; the launch traced here: 67.8 us
  Pallas kernels  67.2 us (99%)
    pallas_call x1, Pallas kernels, shards(): pl.pallas_call(functools.partial(kernel, groups, side, scale), out_shape=...  64.7 us
    pallas_call x1, Pallas kernels, shards(): pl.pallas_call(hand_over, out_shape=shapes, in_specs=[anywhere] * 5, out_...  2.51 us

profile of v7, /device:TPU:1, one launch (start us, length us, event | category | flops | bytes accessed | tf_op | source)
XLA Modules:
  0.0 67.8 jit_solution(12513514223882192980)
XLA Ops:
  0.6 64.7 %shard_map.155 = (bf16[256,1024]{1,0:T(8,128)(2,1)}, bf16[256,1024]{1,0:T(8,128)(2,1)}, bf16[256,1024]{1,0:T(8,128)(2,1)}, bf16[256,1024]{1,0:T(8,128)(2,1)}, f32[64,1024]{1,0:T(8,128)}) custom-call(bf16[256,1024]{1,0:T(8,128)(2,1)} %q_hbm.1, bf16[256,1024]{1,0:T(8,128)(2,1)} %k_hbm.1, bf16[256,1024]{1,0:T(8,128)(2,1)} %v_hbm.1, bf16[256,1024]{1,0:T(8,128)(2,1)} %g_hbm.1, ...), custom_call_target="tpu_custom_call" | custom-call | tf_op jit(solution)/shard_map/pallas_call | solution.py:434
  65.3 2.5 %shard_map.156 = (bf16[256,1024]{1,0:T(8,128)(2,1)}, bf16[256,1024]{1,0:T(8,128)(2,1)}, bf16[256,1024]{1,0:T(8,128)(2,1)}, bf16[256,1024]{1,0:T(8,128)(2,1)}, f32[64,1024]{1,0:T(8,128)}) custom-call(bf16[256,1024]{1,0:T(8,128)(2,1)} %get-tuple-element.10.refs_0_, bf16[256,1024]{1,0:T(8,128)(2,1)} %get-tuple-element.11.refs_1_, ...), custom_call_target="tpu_custom_call" | custom-call | tf_op jit(solution)/shard_map/pallas_call | solution.py:469

commit v8 on v7

--- a/solution.py
+++ b/solution.py
@@ -356,8 +356,6 @@
 
     forth = [(q_ref, out_ref, out_hbm), (g_ref, dq_ref, dq_hbm)]
     back = [(v_ref, dk_ref, dk_hbm), (k_ref, dv_ref, dv_hbm)]
-    wait_all(c0_recv, 4)
-    saves = finish(0, c0_recv, k_ref, v_ref, forth, 0)
     for h in range(2):
         wait_all(r_mid[h], 6 + 8 * h)
         rows = r_mid[h][...].astype(F32)
@@ -366,6 +364,8 @@
             s_send[h * half + z] = level.reshape(side * side * part, span // 2).astype(BF16)
         start_line(s_send, s_recv, 7, h * half)
     s_recv[pl.ds(level_of(mz, upper), 1)] = s_send[pl.ds(mz, 1)]
+    wait_all(c0_recv, 4)
+    saves = finish(0, c0_recv, k_ref, v_ref, forth, 0)
     wait_all(c1_recv, 10)
     saves += finish(1, c1_recv, k_ref, v_ref, forth, 0)
     wait_all(b0_recv, 8)

time: 68 us -> 68 us (level)
  no operation moved by 1% of the time
where the time goes in v8:
time: 68 us; the launch traced here: 67.8 us
  Pallas kernels  67.2 us (99%)
    pallas_call x1, Pallas kernels, shards(): pl.pallas_call(functools.partial(kernel, groups, side, scale), out_shape=...  64.7 us
    pallas_call x1, Pallas kernels, shards(): pl.pallas_call(hand_over, out_shape=shapes, in_specs=[anywhere] * 5, out_...  2.51 us

profile of v8, /device:TPU:1, one launch (start us, length us, event | category | flops | bytes accessed | tf_op | source)
XLA Modules:
  0.0 67.8 jit_solution(8257265594564862703)
XLA Ops:
  0.6 64.7 %shard_map.155 = (bf16[256,1024]{1,0:T(8,128)(2,1)}, bf16[256,1024]{1,0:T(8,128)(2,1)}, bf16[256,1024]{1,0:T(8,128)(2,1)}, bf16[256,1024]{1,0:T(8,128)(2,1)}, f32[64,1024]{1,0:T(8,128)}) custom-call(bf16[256,1024]{1,0:T(8,128)(2,1)} %q_hbm.1, bf16[256,1024]{1,0:T(8,128)(2,1)} %k_hbm.1, bf16[256,1024]{1,0:T(8,128)(2,1)} %v_hbm.1, bf16[256,1024]{1,0:T(8,128)(2,1)} %g_hbm.1, ...), custom_call_target="tpu_custom_call" | custom-call | tf_op jit(solution)/shard_map/pallas_call | solution.py:434
  65.3 2.5 %shard_map.156 = (bf16[256,1024]{1,0:T(8,128)(2,1)}, bf16[256,1024]{1,0:T(8,128)(2,1)}, bf16[256,1024]{1,0:T(8,128)(2,1)}, bf16[256,1024]{1,0:T(8,128)(2,1)}, f32[64,1024]{1,0:T(8,128)}) custom-call(bf16[256,1024]{1,0:T(8,128)(2,1)} %get-tuple-element.10.refs_0_, bf16[256,1024]{1,0:T(8,128)(2,1)} %get-tuple-element.11.refs_1_, ...), custom_call_target="tpu_custom_call" | custom-call | tf_op jit(solution)/shard_map/pallas_call | solution.py:469
